TPU v7x, 256 devices: a whole 4x4x8 slice. The times are simulated.
256 devices in a mesh: rows: 8 (over y, core), cols: 8 (over z), seg: 4 (over x).
Axes of the slice: x: 4, y: 4, z: 8, core: 2. Of those that a mesh axis runs over, the one named last changes fastest.
Arguments:
- right_side: float32 [64, 65536], P(None, ('rows', 'seg'))
- near_blocks: bfloat16 [8, 4, 8, 16, 128, 128], P('rows', 'seg', 'cols'), may hold values from -0.1875 to 0.1875
- near_rows: int32 [8, 4, 8, 16], P('rows', 'seg', 'cols'), may hold values from 0 to 15
- near_cols: int32 [8, 4, 8, 16], P('rows', 'seg', 'cols'), may hold values from 0 to 63
- left_factors: bfloat16 [8, 4, 8, 256, 64, 128], P('rows', 'seg', 'cols'), may hold values from -0.0625 to 0.0625
- right_factors: bfloat16 [8, 4, 8, 256, 64, 128], P('rows', 'seg', 'cols'), may hold values from -0.5 to 0.5
- slot_ranks: int32 [8, 4, 8, 256], P('rows', 'seg', 'cols'), may hold values from 0 to 64, as said below
- slot_rows: int32 [8, 4, 8, 256], P('rows', 'seg', 'cols'), may hold values from 0 to 15
- slot_cols: int32 [8, 4, 8, 256], P('rows', 'seg', 'cols'), may hold values from 0 to 63
Outputs:
- solution: float32 [64, 65536], P(None, ('rows', 'seg'))
- hessen: float32 [192, 128], replicated
Inputs may be any that keep to these rules, and one draw needn't show every extreme that they name: `slot_ranks`: 0 marks an unused slot; the used slots of a device come first and hold ranks of 16 or more; slot 0 has rank 64 on every device.
All inputs are finite; a program needn't handle non-finite values.
Results may differ from a plain program's by a relative error of at most 0.0013.
Values may be sent and summed in bfloat16 or wider, within the bound.
No kernel may reach another device: no remote copies, remote signals or barrier semaphores. Data moves between devices by JAX's collectives and lax.ppermute only.
A program may use at most 64 MiB of HBM per device.

v0:
```python
import jax
import jax.numpy as jnp
from jax import lax
from jax.sharding import PartitionSpec as P

FULL_PRECISION = lax.Precision.HIGHEST


def inner_gram(first_set, second_set):
    return jnp.einsum("ai,bi->ab", first_set, second_set, precision=FULL_PRECISION)


def combine(coeffs, vectors):
    return jnp.einsum("ab,ai->bi", coeffs, vectors, precision=FULL_PRECISION)


def square_of(matrix):
    return jnp.einsum("ab,ac->bc", matrix, matrix, precision=FULL_PRECISION)


def cholesky_upper(gram):
    order = gram.shape[0]
    places = lax.broadcasted_iota(jnp.int32, (order,), 0)

    def cholesky_step_one(column, carry):
        work, upper = carry
        pivot_row = lax.dynamic_slice_in_dim(work, column, 1, 0)[0]
        pivot = lax.dynamic_slice_in_dim(pivot_row, column, 1, 0)[0]
        scaled = jnp.where(places >= column, pivot_row / jnp.sqrt(pivot), 0.0)
        work = work - scaled[:, None] * scaled[None, :]
        marker = (places == column).astype(gram.dtype)
        upper = upper + marker[:, None] * scaled[None, :]
        return (work, upper)

    return lax.fori_loop(0, order, cholesky_step_one, (gram, jnp.zeros_like(gram)))[1]


def upper_inverse(upper):
    order = upper.shape[0]
    places = lax.broadcasted_iota(jnp.int32, (order,), 0)

    def upper_step_one(count, inverse):
        index = order - 1 - count
        row_upper = lax.dynamic_slice_in_dim(upper, index, 1, 0)[0]
        diag_value = lax.dynamic_slice_in_dim(row_upper, index, 1, 0)[0]
        beyond = jnp.where(places > index, row_upper, 0.0)
        marker = (places == index).astype(upper.dtype)
        new_row = (marker - jnp.dot(beyond, inverse, precision=FULL_PRECISION)) / diag_value
        return inverse + marker[:, None] * new_row[None, :]

    return lax.fori_loop(0, order, upper_step_one, jnp.zeros_like(upper))


def chol_parts(gram):
    upper = cholesky_upper(gram)
    return (upper, upper_inverse(upper))


def chol_solve(gram, target):
    inverse = upper_inverse(cholesky_upper(gram))
    return jnp.dot(
        inverse, jnp.dot(inverse.T, target, precision=FULL_PRECISION), precision=FULL_PRECISION
    )


def block_terms(
    panel,
    dense,
    near_rows,
    near_cols,
    left_factors,
    right_factors,
    slot_ranks,
    slot_rows,
    slot_cols,
    clusters,
):
    picked = jnp.take(panel, slot_cols, axis=1)
    coeffs = jnp.einsum("rki,kqi->kqr", picked, right_factors, preferred_element_type=jnp.float32)
    usable = lax.broadcasted_iota(jnp.int32, coeffs.shape[:2], 1) < slot_ranks[:, None]
    coeffs = jnp.where(usable[:, :, None], coeffs, 0.0).astype(jnp.bfloat16)
    low_rank = jnp.einsum("kqr,kqi->kri", coeffs, left_factors, preferred_element_type=jnp.float32)
    nearby = jnp.take(panel, near_cols, axis=1)
    near_part = jnp.einsum("kij,rkj->kri", dense, nearby, preferred_element_type=jnp.float32)
    targets = lax.broadcasted_iota(jnp.int32, (clusters, 1), 0)
    slot_select = (slot_rows[None, :] == targets).astype(jnp.float32)
    near_select = (near_rows[None, :] == targets).astype(jnp.float32)
    total = jnp.einsum("lk,kri->rli", slot_select, low_rank, precision=FULL_PRECISION) + jnp.einsum(
        "lk,kri->rli", near_select, near_part, precision=FULL_PRECISION
    )
    return total.reshape(total.shape[0], -1)


def orthogonalize(basis, image, reduce_sum):
    totals = reduce_sum(jnp.stack([inner_gram(vector_set, image) for vector_set in basis]))
    projections = [totals[index] for index in range(len(basis))]
    for vector_set, coeffs in zip(basis, projections):
        image = image - combine(coeffs, vector_set)
    gram = reduce_sum(inner_gram(image, image)[None])[0]
    return (projections, image, gram)


def solve_block(start, apply_fn, reduce_sum):
    start_factor, start_inverse = chol_parts(reduce_sum(inner_gram(start, start)[None])[0])
    first_basis = combine(start_inverse, start)
    projections, image, gram = orthogonalize([first_basis], apply_fn(first_basis), reduce_sum)
    head_one = projections[0]
    lower_one, lower_inverse = chol_parts(gram)
    second_basis = combine(lower_inverse, image)
    projections, image, gram = orthogonalize(
        [first_basis, second_basis], apply_fn(second_basis), reduce_sum
    )
    cross_one, cross_two = projections
    lower_two = cholesky_upper(gram)
    zero_block = jnp.zeros_like(head_one)
    hessen = jnp.concatenate(
        [
            jnp.concatenate([head_one, cross_one], 1),
            jnp.concatenate([lower_one, cross_two], 1),
            jnp.concatenate([zero_block, lower_two], 1),
        ],
        0,
    )
    target = jnp.concatenate(
        [
            jnp.dot(head_one.T, start_factor, precision=FULL_PRECISION),
            jnp.dot(cross_one.T, start_factor, precision=FULL_PRECISION),
        ],
        0,
    )
    weights = chol_solve(square_of(hessen), target)
    width_rhs = head_one.shape[0]
    solution = combine(weights[:width_rhs], first_basis) + combine(
        weights[width_rhs:], second_basis
    )
    return (solution, hessen)


def body(
    right_side,
    near_blocks,
    near_rows,
    near_cols,
    left_factors,
    right_factors,
    slot_ranks,
    slot_rows,
    slot_cols,
):
    col_count = lax.axis_size("cols")
    col_index = lax.axis_index("cols")
    width_rhs = right_side.shape[0]
    leaf_cells = near_blocks.shape[-1]
    clusters = right_side.shape[1] // leaf_cells
    group = clusters // col_count
    operator = (
        near_blocks.reshape(near_blocks.shape[3:]),
        near_rows.reshape(-1),
        near_cols.reshape(-1),
        left_factors.reshape(left_factors.shape[3:]),
        right_factors.reshape(right_factors.shape[3:]),
        slot_ranks.reshape(-1),
        slot_rows.reshape(-1),
        slot_cols.reshape(-1),
    )

    def local_terms(share):
        panel = lax.all_gather(share, ("rows", "seg"), axis=1, tiled=True)
        panel = panel.reshape(width_rhs, panel.shape[1] // leaf_cells, leaf_cells)
        return block_terms(panel, *operator, clusters)

    def reduce_sum(values):
        return lax.psum(values, ("rows", "seg"))

    def apply_fn(vectors):
        share = lax.dynamic_slice_in_dim(
            vectors, col_index * group * leaf_cells, group * leaf_cells, 1
        )
        terms = local_terms(share.astype(jnp.bfloat16))
        return lax.psum(terms, "cols") + 0.5 * vectors

    solution, hessen = solve_block(right_side, apply_fn, reduce_sum)
    return (solution, hessen)


def solution(mesh):
    in_specs = (
        P(None, ("rows", "seg")),
        P("rows", "seg", "cols", None, None, None),
        P("rows", "seg", "cols", None),
        P("rows", "seg", "cols", None),
        P("rows", "seg", "cols", None, None, None),
        P("rows", "seg", "cols", None, None, None),
        P("rows", "seg", "cols", None),
        P("rows", "seg", "cols", None),
        P("rows", "seg", "cols", None),
    )
    out_specs = (P(None, ("rows", "seg")), P())
    return jax.shard_map(body, mesh=mesh, in_specs=in_specs, out_specs=out_specs, check_vma=False)
```

profile of v0, /device:TPU:1, one launch (start us, length us, event | category | flops | bytes accessed | tf_op | source)
XLA Modules:
  0.0 1797.9 jit_solution(11197933853168069760)
XLA Ops:
  7.3 1.8 fusion.143
  9.1 124.9 %psum.49 = f32[64,64]{1,0:T(8,128)S(1)} all-reduce(f32[64,64]{1,0:T(8,128)S(1)} %fusion.143), channel_id=1, replica_groups=mesh['rows'=8,'cols'=8,'seg'=4] {'rows','seg'}, use_global_device_ids=true, to_apply=%region_0.0 | all-reduce | flops 4096 | bytes 32768 | tf_op jit(solution)/shard_map/psum | solution.py:173
  134.0 94.6 %while.134 = (s32[]{:T(128)}, f32[64,64]{1,0:T(8,128)S(1)}, f32[64,64]{1,0:T(8,128)S(1)}, s32[]{:T(128)}, s32[]{:T(128)}, /*index=5*/s32[]{:T(128)}) while((s32[]{:T(128)}, f32[64,64]{1,0:T(8,128)S(1)}, f32[64,64]{1,0:T(8,128)S(1)}, s32[]{:T(128)}, s32[]{:T(128)}, /*index=5*/s32[]{:T(128)}) %tuple.323), condition=%wide.region_2.3_spmd.clone.clone, body=%wide.region_1.2_spmd.clone.clone.sunk | while | flops 20932 | bytes 68999 | solution.py:35
  228.5 93.7 %while.135 = (s32[]{:T(128)}, f32[64,64]{1,0:T(8,128)S(1)}, f32[64,64]{1,0:T(8,128)S(1)}, s32[]{:T(128)}, s32[]{:T(128)}, /*index=5*/s32[]{:T(128)}, s32[]{:T(128)}) while((s32[]{:T(128)}, f32[64,64]{1,0:T(8,128)S(1)}, f32[64,64]{1,0:T(8,128)S(1)}, s32[]{:T(128)}, s32[]{:T(128)}, /*index=5*/s32[]{:T(128)}, ...), condition=%wide.region_4.5_spmd.clone.clone, body=%wide.region_3.4_spmd.clone.clone.sunk | while | flops 66056 | bytes 69297 | solution.py:51
  322.2 1.7 fusion.144
  328.1 47.2 %all-gather.3.cloned.1.call-done = bf16[64,8192]{1,0:T(8,128)(2,1)} async-done(((bf16[64,256]{1,0:T(8,128)(2,1)}), bf16[64,8192]{1,0:T(8,128)(2,1)}) %all-gather.3.cloned.1.call-update) | async-done | bytes 1048592 | tf_op jit(solution)/shard_map/all_gather | solution.py:168
  375.3 1.5 copy_bitcast_fusion.1
  377.4 3.1 gather_fusion
  380.5 11.4 fusion.61
  391.8 10.4 fusion.59
  402.8 0.9 convolution_add_fusion.2
  403.7 1.0 copy.40
  404.7 67.9 %all-reduce.4.cloned.1.call-done = f32[64,2048]{1,0:T(8,128)} async-done(((f32[64,2048]{1,0:T(8,128)}), f32[64,2048]{1,0:T(8,128)}) %all-reduce.4.cloned.1.call-update) | async-done | bytes 524304 | tf_op jit(solution)/shard_map/psum | solution.py:180
  472.6 1.6 fusion.103
  474.3 125.5 %psum.51 = f32[64,64]{1,0:T(8,128)S(1)} all-reduce(f32[64,64]{1,0:T(8,128)S(1)} %fusion.103), channel_id=1, replica_groups=mesh['rows'=8,'cols'=8,'seg'=4] {'rows','seg'}, use_global_device_ids=true, to_apply=%region_6.9 | all-reduce | flops 4096 | bytes 32768 | tf_op jit(solution)/shard_map/psum | solution.py:173
  599.7 1.7 convolution_subtract_fusion.2
  602.0 124.1 %psum.52 = f32[64,64]{1,0:T(8,128)S(1)} all-reduce(f32[64,64]{1,0:T(8,128)S(1)} %fusion.145), channel_id=1, replica_groups=mesh['rows'=8,'cols'=8,'seg'=4] {'rows','seg'}, use_global_device_ids=true, to_apply=%region_7.10 | all-reduce | flops 4096 | bytes 32768 | tf_op jit(solution)/shard_map/psum | solution.py:173
  726.1 92.1 %while.136 = (s32[]{:T(128)}, f32[64,64]{1,0:T(8,128)S(1)}, f32[64,64]{1,0:T(8,128)S(1)}, s32[]{:T(128)}, s32[]{:T(128)}, /*index=5*/s32[]{:T(128)}) while((s32[]{:T(128)}, f32[64,64]{1,0:T(8,128)S(1)}, f32[64,64]{1,0:T(8,128)S(1)}, s32[]{:T(128)}, s32[]{:T(128)}, /*index=5*/s32[]{:T(128)}) %tuple.329), condition=%wide.region_9.12_spmd.clone.clone, body=%wide.region_8.11_spmd.clone.clone.sunk | while | flops 20932 | bytes 68999 | solution.py:35
  818.2 93.7 %while.137 = (s32[]{:T(128)}, f32[64,64]{1,0:T(8,128)S(1)}, f32[64,64]{1,0:T(8,128)S(1)}, s32[]{:T(128)}, s32[]{:T(128)}, /*index=5*/s32[]{:T(128)}, s32[]{:T(128)}) while((s32[]{:T(128)}, f32[64,64]{1,0:T(8,128)S(1)}, f32[64,64]{1,0:T(8,128)S(1)}, s32[]{:T(128)}, s32[]{:T(128)}, /*index=5*/s32[]{:T(128)}, ...), condition=%wide.region_11.14_spmd.clone.clone, body=%wide.region_10.13_spmd.clone.clone.sunk | while | flops 66056 | bytes 69297 | solution.py:51
  913.2 46.1 %all-gather.5.cloned.1.call-done = bf16[64,8192]{1,0:T(8,128)(2,1)} async-done(((bf16[64,256]{1,0:T(8,128)(2,1)}), bf16[64,8192]{1,0:T(8,128)(2,1)}) %all-gather.5.cloned.1.call-update) | async-done | bytes 1048592 | tf_op jit(solution)/shard_map/all_gather | solution.py:168
  959.3 1.5 copy_bitcast_fusion
  961.4 3.1 gather_fusion.2
  965.0 11.3 fusion.62
  976.3 10.4 fusion.57
  986.7 0.9 convolution_add_fusion.1
  987.6 1.0 copy.39
  988.9 67.7 %all-reduce.6.cloned.1.call-done = f32[64,2048]{1,0:T(8,128)} async-done(((f32[64,2048]{1,0:T(8,128)}), f32[64,2048]{1,0:T(8,128)}) %all-reduce.6.cloned.1.call-update) | async-done | bytes 524304 | tf_op jit(solution)/shard_map/psum | solution.py:180
  1056.6 1.6 convolution_bitcast_fusion.3
  1058.2 1.6 convolution_bitcast_fusion.4
  1059.9 125.5 %psum.54 = f32[2,64,64]{2,1,0:T(8,128)S(1)} all-reduce(f32[2,64,64]{2,1,0:T(8,128)S(1)} %pad_maximum_fusion), channel_id=1, replica_groups=mesh['rows'=8,'cols'=8,'seg'=4] {'rows','seg'}, use_global_device_ids=true, to_apply=%region_13.16 | all-reduce | flops 8192 | bytes 65536 | tf_op jit(solution)/shard_map/psum | solution.py:173
  1185.6 1.7 convolution_subtract_fusion.1
  1188.5 124.1 %psum.55 = f32[64,64]{1,0:T(8,128)S(1)} all-reduce(f32[64,64]{1,0:T(8,128)S(1)} %fusion.147), channel_id=1, replica_groups=mesh['rows'=8,'cols'=8,'seg'=4] {'rows','seg'}, use_global_device_ids=true, to_apply=%region_14.17 | all-reduce | flops 4096 | bytes 32768 | tf_op jit(solution)/shard_map/psum | solution.py:173
  1312.6 92.1 %while.138 = (s32[]{:T(128)}, f32[64,64]{1,0:T(8,128)S(1)}, f32[64,64]{1,0:T(8,128)S(1)}, s32[]{:T(128)}, s32[]{:T(128)}, /*index=5*/s32[]{:T(128)}) while((s32[]{:T(128)}, f32[64,64]{1,0:T(8,128)S(1)}, f32[64,64]{1,0:T(8,128)S(1)}, s32[]{:T(128)}, s32[]{:T(128)}, /*index=5*/s32[]{:T(128)}) %tuple.335), condition=%wide.region_16.19_spmd.clone.clone, body=%wide.region_15.18_spmd.clone.clone.sunk | while | flops 20932 | bytes 68999 | solution.py:35
  1405.3 187.6 %while.139 = (s32[]{:T(128)}, f32[128,128]{1,0:T(8,128)S(1)}, f32[128,128]{1,0:T(8,128)S(1)}, s32[]{:T(128)}, s32[]{:T(128)}, /*index=5*/s32[]{:T(128)}) while((s32[]{:T(128)}, f32[128,128]{1,0:T(8,128)S(1)}, f32[128,128]{1,0:T(8,128)S(1)}, s32[]{:T(128)}, s32[]{:T(128)}, /*index=5*/s32[]{:T(128)}) %tuple.338), condition=%wide.region_18.21_spmd.clone.clone, body=%wide.region_17.20_spmd.clone.clone.sunk | while | flops 82820 | bytes 267911 | solution.py:35
  1592.8 196.0 %while.140 = (s32[]{:T(128)}, f32[128,128]{1,0:T(8,128)S(1)}, f32[128,128]{1,0:T(8,128)S(1)}, s32[]{:T(128)}, s32[]{:T(128)}, /*index=5*/s32[]{:T(128)}, s32[]{:T(128)}) while((s32[]{:T(128)}, f32[128,128]{1,0:T(8,128)S(1)}, f32[128,128]{1,0:T(8,128)S(1)}, s32[]{:T(128)}, s32[]{:T(128)}, /*index=5*/s32[]{:T(128)}, ...), condition=%wide.region_20.23_spmd.clone.clone, body=%wide.region_19.22_spmd.clone.clone.sunk | while | flops 263176 | bytes 201393 | solution.py:51
  1593.4 0.8 fusion.205
  1595.0 0.8 fusion.205
  1614.9 0.8 fusion.205
  1616.4 0.8 fusion.205
  1617.9 0.8 fusion.205
  1619.5 0.8 fusion.205
  1621.0 0.8 fusion.205
  1622.5 0.8 fusion.205
  1624.1 0.8 fusion.205
  1644.0 0.8 fusion.205
  1645.5 0.8 fusion.205
  1647.0 0.8 fusion.205
  1648.6 0.8 fusion.205
  1650.1 0.8 fusion.205
  1651.6 0.8 fusion.205
  1653.2 0.8 fusion.205
  1673.1 0.8 fusion.205
  1674.6 0.8 fusion.205
  1676.1 0.8 fusion.205
  1677.7 0.8 fusion.205
  1679.2 0.8 fusion.205
  1680.7 0.8 fusion.205
  1682.3 0.8 fusion.205
  1702.2 0.8 fusion.205
  1703.7 0.8 fusion.205
  1705.2 0.8 fusion.205
  1706.8 0.8 fusion.205
  1708.3 0.8 fusion.205
  1789.9 1.4 convolution_add_fusion
  (2645 shorter events, 597.3 us)
Async XLA Ops:
  7.2 395.1 %copy-start = (bf16[1,1,1,16,128,128]{5,4,3,2,1,0:T(8,128)(2,1)S(1)}, bf16[1,1,1,16,128,128]{5,4,3,2,1,0:T(8,128)(2,1)}, u32[]{:S(2)}) copy-start(bf16[1,1,1,16,128,128]{5,4,3,2,1,0:T(8,128)(2,1)} %param.28) | copy-start | bytes 1572868
  7.2 368.1 %all-gather.3.cloned.1.call-start = ((), (), s32[]{:S(2)}) async-start(), calls=%async_computation | async-start | bytes 1081344 | tf_op jit(solution)/shard_map/all_gather | solution.py:168
  324.6 148.1 %all-reduce.4.cloned.1.call-start = ((), (), s32[]{:S(2)}) async-start(), calls=%async_computation.1 | async-start | bytes 1048576 | tf_op jit(solution)/shard_map/psum | solution.py:180
  380.5 11.4 copy-start.2
  391.8 10.9 copy-start.3
  404.6 554.6 %all-gather.5.cloned.1.call-start = ((), (), s32[]{:S(2)}) async-start(), calls=%async_computation.2 | async-start | bytes 1081344 | tf_op jit(solution)/shard_map/all_gather | solution.py:168
  913.2 143.5 %all-reduce.6.cloned.1.call-start = ((), (), s32[]{:S(2)}) async-start(), calls=%async_computation.3 | async-start | bytes 1048576 | tf_op jit(solution)/shard_map/psum | solution.py:180
  1404.8 386.6 %copy-start.1 = (f32[192,128]{1,0:T(8,128)}, f32[192,128]{1,0:T(8,128)S(1)}, u32[]{:S(2)}) copy-start(f32[192,128]{1,0:T(8,128)S(1)} %select_maximum_fusion) | copy-start | bytes 294916
Sparse Core Ops, SparseCore 0:
  324.7 50.5 all-gather.2
  404.8 67.8 all-reduce.3
  913.3 45.9 all-gather.4
  988.7 67.8 all-reduce.5
where the time goes:
time: 1810 us; the launch traced here: 1800 us
  blocking collectives  624 us (34%)
  local copies, waits for them, and re-layouts  357 us (20%)
  matrix products  267 us (15%)
  loops' own time  242 us (13%)
  waiting for transfers between devices  229 us (13%)
  other arithmetic  65.2 us (4%)
    psum x5, blocking collectives, reduce_sum(): return lax.psum(values, ('rows', 'seg'))  624 us
    another operation x4, loops' own time, cholesky_upper(): lax.fori_loop(0, order, cholesky_step_one, (gram, jnp.zeros_like(gram)))[1]  236 us
    dot_general x256, matrix products, upper_step_one(): jnp.dot(beyond, inverse, precision=FULL_PRECISION)  203 us
    dynamic_slice x320, local copies, waits for them, and re-layouts, cholesky_step_one(): pivot = lax.dynamic_slice_in_dim(pivot_row, column, 1, 0)[0]  192 us
    dynamic_slice x256, local copies, waits for them, and re-layouts, upper_step_one(): diag_value = lax.dynamic_slice_in_dim(row_upper, index, 1, 0)[0]  151 us
    psum x2, waiting for transfers between devices, apply_fn(): return lax.psum(terms, 'cols') + 0.5 * vectors  136 us
    all_gather x2, waiting for transfers between devices, local_terms(): panel = lax.all_gather(share, ('rows', 'seg'), axis=1, tiled=True)  93.3 us
  transfers between devices with their start and end apart: 4, of which 4 were waited for; matrix products, arithmetic and copies ran while one was open for 0% of the time, Pallas kernels for 0%

commit v1 on v0

v1 whole, which is shorter than its diff:
```python
import functools

import jax
import jax.numpy as jnp
from jax import lax
from jax.experimental import pallas as pl
from jax.experimental.pallas import tpu as pltpu
from jax.sharding import PartitionSpec as P

FULL = lax.Precision.HIGHEST
NN = (((1,), (0,)), ((), ()))
NT = (((1,), (1,)), ((), ()))
TN = (((0,), (0,)), ((), ()))
CHUNKS = 8
UNROLL = 8
VMEM_LIMIT = 48 * 1024 * 1024


def mm(a, b, dims=NN):
    return lax.dot_general(a, b, dims, precision=FULL, preferred_element_type=jnp.float32)


def vmem():
    return pl.BlockSpec(memory_space=pltpu.VMEM)


def smem():
    return pl.BlockSpec(memory_space=pltpu.SMEM)


def eye(order):
    rows = lax.broadcasted_iota(jnp.int32, (order, order), 0)
    cols = lax.broadcasted_iota(jnp.int32, (order, order), 1)
    return (rows == cols).astype(jnp.float32)


def eliminate(works):
    order = works[0].shape[0]
    works = list(works)
    for k in range(order):
        base = (k // 8) * 8
        for at, work in enumerate(works):
            pivot_row = work[k : k + 1, :]
            ratio = pivot_row * (1.0 / pivot_row[:, k : k + 1])
            low = work[base:, :]
            places = lax.broadcasted_iota(jnp.int32, (order - base, 1), 0) + base
            factor = jnp.where(places > k, low[:, k : k + 1], 0.0)
            low = low - factor * ratio
            works[at] = low if base == 0 else jnp.concatenate([work[:base], low], 0)
    results = []
    for work in works:
        rows = lax.broadcasted_iota(jnp.int32, work.shape, 0)
        cols = lax.broadcasted_iota(jnp.int32, work.shape, 1)
        diagonal = jnp.sum(jnp.where(rows == cols, work, 0.0), axis=1, keepdims=True)
        scaled = work * (1.0 / jnp.sqrt(diagonal))
        results.append(jnp.where(cols >= rows, scaled, jnp.where(cols >= order, scaled, 0.0)))
    return results


def start_gram_kernel(piece_ref, gram_ref):
    piece = piece_ref[...]
    gram_ref[...] = mm(piece, piece, NT)


def start_factor_kernel(gram_ref, factor_ref, inverse_ref):
    order = gram_ref.shape[0]
    (done,) = eliminate([jnp.concatenate([gram_ref[...], eye(order)], 1)])
    factor_ref[...] = done[:, :order]
    inverse_ref[...] = done[:, order:]


def share_gram_kernel(count, *refs):
    bases, terms_ref, share_ref, gram_ref = refs[:count], refs[count], refs[count + 1], refs[count + 2]
    share = terms_ref[0]
    for index in range(1, terms_ref.shape[0]):
        share = share + terms_ref[index]
    share_ref[...] = share
    order = share.shape[1]
    for at in range(count + 1):
        total = None
        for half in range(share.shape[0]):
            left = share[half] if at == count else bases[at][half]
            product = mm(left, share[half], NT)
            total = product if total is None else total + product
        gram_ref[at * order : (at + 1) * order, :] = total


def sum_leading(ref):
    total = ref[0]
    for index in range(1, ref.shape[0]):
        total = total + ref[index]
    return total


def middle_kernel(grams_ref, head_ref, lower_ref, first_ref, second_ref):
    totals = sum_leading(grams_ref)
    order = totals.shape[1]
    cross, square = totals[:order], totals[order:]
    gram = square - mm(cross, cross, TN)
    (done,) = eliminate([jnp.concatenate([gram, eye(order)], 1)])
    inverse = done[:, order:]
    head_ref[...] = cross + 0.5 * eye(order)
    lower_ref[...] = done[:, :order]
    first_ref[...] = inverse
    second_ref[...] = -mm(inverse, cross, NT)


def final_kernel(
    grams_ref, start_ref, head_ref, lower_ref, own_ref, mix_ref, base_ref, hessen_ref, w_right_ref, w_image_ref
):
    totals = sum_leading(grams_ref)
    order = totals.shape[1]
    unit = eye(order)
    cross_one = totals[:order]
    inner = totals[order : 2 * order]
    cross_two = inner + 0.5 * unit
    gram = totals[2 * order :] - mm(cross_one, cross_one, TN) - mm(inner, inner, TN)
    start, head, lower = start_ref[...], head_ref[...], lower_ref[...]
    top = mm(head, head, TN) + mm(lower, lower, TN)
    side = mm(head, cross_one, TN) + mm(lower, cross_two, TN)
    corner = mm(cross_one, cross_one, TN) + mm(cross_two, cross_two, TN) + gram
    upper_target = mm(head, start, TN)
    lower_target = mm(cross_one, start, TN)
    pad = jnp.zeros_like(gram)
    top_done, gram_done = eliminate(
        [jnp.concatenate([top, unit, side, upper_target], 1), jnp.concatenate([gram, pad], 1)]
    )
    inverse_top = top_done[:, order : 2 * order]
    bridge = top_done[:, 2 * order : 3 * order]
    part = top_done[:, 3 * order :]
    schur = corner - mm(bridge, bridge, TN)
    (low_done,) = eliminate(
        [jnp.concatenate([schur, unit, lower_target - mm(bridge, part, TN), pad], 1)]
    )
    low_weights = mm(low_done[:, order : 2 * order], low_done[:, 2 * order : 3 * order], TN)
    top_weights = mm(inverse_top, part - mm(bridge, low_weights), TN)
    hessen_ref[:order, :order] = head
    hessen_ref[:order, order:] = cross_one
    hessen_ref[order : 2 * order, :order] = lower
    hessen_ref[order : 2 * order, order:] = cross_two
    hessen_ref[2 * order :, :order] = pad
    hessen_ref[2 * order :, order:] = gram_done[:, :order]
    w_image_ref[...] = mm(low_weights, own_ref[...], TN)
    first = top_weights + mm(mix_ref[...], low_weights, TN)
    w_right_ref[...] = mm(first, base_ref[...], TN)


def solution_kernel(w_right_ref, w_image_ref, right_ref, image_ref, out_ref):
    leaf = image_ref.shape[-1]
    for cluster in range(image_ref.shape[0] * image_ref.shape[1]):
        cells = pl.ds(cluster * leaf, leaf)
        group = image_ref.shape[1]
        out_ref[:, cells] = mm(w_right_ref[...], right_ref[:, cells]) + mm(
            w_image_ref[...], image_ref[cluster // group, cluster % group]
        )


def apply_kernel(
    panels,
    keep_all,
    near_rows_ref,
    near_cols_ref,
    ranks_ref,
    rows_ref,
    cols_ref,
    *refs,
):
    mixes, refs = refs[:panels], refs[panels:]
    panel_refs, refs = refs[: 2 * panels], refs[2 * panels :]
    near_hbm, left_hbm, right_hbm, basis_ref, terms_ref = refs[:5]
    rounded, near, left, right, sems, near_sem = refs[5:]
    slots = left.shape[0]
    per = slots // CHUNKS
    copies = []
    near_copy = pltpu.make_async_copy(near_hbm, near, near_sem)
    near_copy.start()
    for chunk in range(CHUNKS):
        part = pl.ds(chunk * per, per)
        pair = (
            pltpu.make_async_copy(right_hbm.at[part], right.at[part], sems.at[chunk, 0]),
            pltpu.make_async_copy(left_hbm.at[part], left.at[part], sems.at[chunk, 1]),
        )
        for copy in pair:
            copy.start()
        copies.append(pair)
    terms_ref[...] = jnp.zeros_like(terms_ref)
    half_count = panel_refs[0].shape[0]
    group = terms_ref.shape[1]
    coeffs = [mix[...] for mix in mixes]
    for side in range(2):
        offset = side * half_count

        def make_basis(index, _, side=side, offset=offset):
            value = mm(coeffs[0], panel_refs[side][index])
            for at in range(1, panels):
                value = value + mm(coeffs[at], panel_refs[2 * at + side][index])
            rounded[offset + index] = value.astype(jnp.bfloat16)
            if keep_all:
                basis_ref[offset + index] = value
            elif side == 0:

                @pl.when(index < group)
                def _():
                    basis_ref[index] = value

            return 0

        lax.fori_loop(0, half_count, make_basis, 0, unroll=4)

    near_copy.wait()
    order = rounded.shape[1]
    columns = lax.broadcasted_iota(jnp.int32, (order, left.shape[1]), 1)

    def add_to(row, value):
        terms_ref[row // group, row % group] += value

    def near_step(step, _):
        values = []
        for inner in range(4):
            at = step * 4 + inner
            values.append(
                lax.dot_general(
                    rounded[near_cols_ref[at]], near[at], NT, preferred_element_type=jnp.float32
                )
            )
        for inner, value in enumerate(values):
            add_to(near_rows_ref[step * 4 + inner], value)
        return 0

    lax.fori_loop(0, near.shape[0] // 4, near_step, 0)

    def slot_step(step, _):
        coefs = []
        for inner in range(UNROLL):
            at = step * UNROLL + inner
            coef = lax.dot_general(
                rounded[cols_ref[at]], right[at], NT, preferred_element_type=jnp.float32
            )
            coefs.append(jnp.where(columns < ranks_ref[at], coef, 0.0).astype(jnp.bfloat16))
        values = []
        for inner in range(UNROLL):
            values.append(
                lax.dot_general(
                    coefs[inner], left[step * UNROLL + inner], NN, preferred_element_type=jnp.float32
                )
            )
        for inner, value in enumerate(values):
            add_to(rows_ref[step * UNROLL + inner], value)
        return 0

    for chunk in range(CHUNKS):
        for copy in copies[chunk]:
            copy.wait()
        lax.fori_loop(chunk * per // UNROLL, (chunk + 1) * per // UNROLL, slot_step, 0)


def apply_operator(mixes, halves, operator, keep_all, shape_of_terms):
    near, near_rows, near_cols, left, right, ranks, rows, cols = operator
    order, leaf = shape_of_terms[2], shape_of_terms[3]
    clusters = 2 * halves[0].shape[0]
    kept = clusters if keep_all else shape_of_terms[1]
    operands = [near_rows, near_cols, ranks, rows, cols, *mixes, *halves, near, left, right]
    specs = [smem()] * 5 + [vmem()] * (len(mixes) + len(halves)) + [pl.BlockSpec(memory_space=pl.ANY)] * 3
    return pl.pallas_call(
        functools.partial(apply_kernel, len(mixes), keep_all),
        out_shape=(
            jax.ShapeDtypeStruct((kept, order, leaf), jnp.float32),
            jax.ShapeDtypeStruct(shape_of_terms, jnp.float32),
        ),
        in_specs=specs,
        out_specs=(vmem(), vmem()),
        scratch_shapes=[
            pltpu.VMEM((clusters, order, leaf), jnp.bfloat16),
            pltpu.VMEM(near.shape, near.dtype),
            pltpu.VMEM(left.shape, left.dtype),
            pltpu.VMEM(right.shape, right.dtype),
            pltpu.SemaphoreType.DMA((CHUNKS, 2)),
            pltpu.SemaphoreType.DMA,
        ],
        compiler_params=pltpu.CompilerParams(vmem_limit_bytes=VMEM_LIMIT),
    )(*operands)


def call(kernel, outs, *operands):
    return pl.pallas_call(
        kernel,
        out_shape=tuple(jax.ShapeDtypeStruct(shape, jnp.float32) for shape in outs),
        in_specs=[vmem()] * len(operands),
        out_specs=tuple(vmem() for _ in outs),
        compiler_params=pltpu.CompilerParams(vmem_limit_bytes=VMEM_LIMIT),
    )(*operands)


def exchange(values, axis, distance):
    count = lax.axis_size(axis)
    return lax.ppermute(values, axis, [(at, at ^ distance) for at in range(count)])


SEG_STEPS = ("seg", (1, 2, 3))
CHIP_STEPS = ("rows", (2, 4, 6))


def reduce_rows_seg(values):
    for axis, steps in (SEG_STEPS, CHIP_STEPS):
        one, two, three = [exchange(values, axis, step) for step in steps]
        values = (values + one) + (two + three)
    return values + exchange(values, "rows", 1)


def gather_halves(share):
    for axis, steps in (SEG_STEPS, CHIP_STEPS):
        share = jnp.concatenate([share] + [exchange(share, axis, step) for step in steps], 0)
    return [share, exchange(share, "rows", 1)]


def spread_cols(values):
    count = lax.axis_size("cols")
    return lax.all_to_all(jnp.broadcast_to(values[None], (count,) + values.shape), "cols", 0, 0)


def body(
    right_side,
    near_blocks,
    near_rows,
    near_cols,
    left_factors,
    right_factors,
    slot_ranks,
    slot_rows,
    slot_cols,
):
    col_count = lax.axis_size("cols")
    col_index = lax.axis_index("cols")
    order, cells = right_side.shape
    leaf = near_blocks.shape[-1]
    group = cells // leaf // col_count
    me = lax.axis_index("rows") * lax.axis_size("seg") + lax.axis_index("seg")

    def relative(columns):
        piece = (columns.reshape(-1) // group) ^ me
        place = ((piece >> 3) & 3) * 4 + ((piece >> 2) & 1) * 16 + (piece & 3)
        return place * group + columns.reshape(-1) % group

    operator = (
        near_blocks.reshape(near_blocks.shape[3:]),
        near_rows.reshape(-1),
        relative(near_cols),
        left_factors.reshape(left_factors.shape[3:]),
        right_factors.reshape(right_factors.shape[3:]),
        slot_ranks.reshape(-1),
        slot_rows.reshape(-1),
        relative(slot_cols),
    )
    square = (order, order)
    share_shape = (group, order, leaf)
    terms_shape = (col_count,) + share_shape

    share = lax.dynamic_slice_in_dim(right_side, col_index * group * leaf, group * leaf, 1)
    share = jnp.transpose(share.reshape(order, group, leaf), (1, 0, 2))
    start_halves = gather_halves(share)
    (gram,) = call(start_gram_kernel, [square], right_side)
    gram = reduce_rows_seg(gram)
    start_factor, base = call(start_factor_kernel, [square, square], gram)

    first_panel, terms = apply_operator([base], start_halves, operator, True, terms_shape)
    first_share = first_panel[:group]
    received = lax.all_to_all(terms, "cols", 0, 0)
    image, grams = call(
        functools.partial(share_gram_kernel, 1), [share_shape, (2 * order, order)], first_share, received
    )
    image_halves = gather_halves(image)
    image_piece = spread_cols(image)
    grams = spread_cols(reduce_rows_seg(grams))
    head, lower, own, mix = call(middle_kernel, [square] * 4, grams)

    half = first_panel.shape[0] // 2
    second_share, terms = apply_operator(
        [own, mix], image_halves + [first_panel[:half], first_panel[half:]], operator, False, terms_shape
    )
    received = lax.all_to_all(terms, "cols", 0, 0)
    _, grams = call(
        functools.partial(share_gram_kernel, 2),
        [share_shape, (3 * order, order)],
        first_share,
        second_share,
        received,
    )
    grams = spread_cols(reduce_rows_seg(grams))
    hessen, w_right, w_image = call(
        final_kernel,
        [(3 * order, 2 * order), square, square],
        grams,
        start_factor,
        head,
        lower,
        own,
        mix,
        base,
    )
    (answer,) = call(solution_kernel, [(order, cells)], w_right, w_image, right_side, image_piece)
    return (answer, hessen)


def solution(mesh):
    in_specs = (
        P(None, ("rows", "seg")),
        P("rows", "seg", "cols", None, None, None),
        P("rows", "seg", "cols", None),
        P("rows", "seg", "cols", None),
        P("rows", "seg", "cols", None, None, None),
        P("rows", "seg", "cols", None, None, None),
        P("rows", "seg", "cols", None),
        P("rows", "seg", "cols", None),
        P("rows", "seg", "cols", None),
    )
    out_specs = (P(None, ("rows", "seg")), P())
    return jax.shard_map(body, mesh=mesh, in_specs=in_specs, out_specs=out_specs, check_vma=False)
```

time: 1810 us -> 274 us (0.15)
  blocking collectives: 624 us -> 40.8 us
  local copies, waits for them, and re-layouts: 357 us -> 18.5 us
  matrix products: 267 us -> 0 us
  loops' own time: 242 us -> 0 us
  waiting for transfers between devices: 229 us -> 79.4 us
  Pallas kernels: 0 us -> 67.2 us
  starting transfers between devices: 0.16 us -> 64.3 us
  other arithmetic: 65.2 us -> 1.51 us
    psum x5 -> x0, blocking collectives: 624 us -> none  [reduce_sum(): return lax.psum(values, ('rows', 'seg'))]
    dynamic_slice x576 -> x0, local copies, waits for them, and re-layouts: 344 us -> none  [the longest x320 192 us: cholesky_step_one(): pivot = lax.dynamic_slice_in_dim(pivot_row, column, 1, 0)[0]]
    dot_general x282 -> x0, matrix products: 267 us -> none  [the longest x256 203 us: upper_step_one(): jnp.dot(beyond, inverse, precision=FULL_PRECISION)]
    another operation x7 -> x0, loops' own time: 242 us -> none  [the longest x4 236 us: cholesky_upper(): lax.fori_loop(0, order, cholesky_step_one, (gram, jnp.zeros_like(gram)))[1]]
    psum x2 -> x0, waiting for transfers between devices: 136 us -> none  [apply_fn(): return lax.psum(terms, 'cols') + 0.5 * vectors]
    all_gather x2 -> x0, waiting for transfers between devices: 93.3 us -> none  [local_terms(): panel = lax.all_gather(share, ('rows', 'seg'), axis=1, tiled=True)]
    pallas_call x0 -> x9, Pallas kernels: none -> 67.2 us  [the longest x2 38.9 us: apply_operator(): pl.pallas_call(functools.partial(apply_kernel, len(mixes), keep_all), out...]
    add x576 -> x11, other arithmetic: 53.7 us -> 1.49 us  [the longest x2 1.37 us: relative(): return place * group + columns.reshape(-1) % group]
  transfers between devices with their start and end apart: 4 -> 38, of which waited for: 4 -> 27; matrix products, arithmetic and copies ran while one was open for 0% -> 4% of each run, Pallas kernels for 0% -> 9%
where the time goes in v1:
time: 274 us; the launch traced here: 273 us
  waiting for transfers between devices  79.4 us (29%)
  Pallas kernels  67.2 us (25%)
  starting transfers between devices  64.3 us (23%)
  blocking collectives  40.8 us (15%)
  local copies, waits for them, and re-layouts  18.5 us (7%)
    ppermute x35, starting transfers between devices, exchange(): lax.ppermute(values, axis, [(at, at ^ distance) for at in range(count)])  48.6 us
    ppermute x35, waiting for transfers between devices, exchange(): lax.ppermute(values, axis, [(at, at ^ distance) for at in range(count)])  46.8 us
    pallas_call x2, Pallas kernels, apply_operator(): pl.pallas_call(functools.partial(apply_kernel, len(mixes), keep_all), out...  38.9 us
    pallas_call x7, Pallas kernels, call(): pl.pallas_call(kernel, out_shape=tuple((jax.ShapeDtypeStruct(shape, jnp.f...  28.3 us
    all_to_all x1, blocking collectives, body(): received = lax.all_to_all(terms, 'cols', 0, 0)  20.4 us
    all_to_all x1, blocking collectives, spread_cols(): lax.all_to_all(jnp.broadcast_to(values[None], (count,) + values.shape), '...  20.4 us
    all_to_all x1, waiting for transfers between devices, body(): received = lax.all_to_all(terms, 'cols', 0, 0)  17.9 us
    all_to_all x2, waiting for transfers between devices, spread_cols(): lax.all_to_all(jnp.broadcast_to(values[None], (count,) + values.shape), '...  14.7 us
  transfers between devices with their start and end apart: 38, of which 27 were waited for; matrix products, arithmetic and copies ran while one was open for 4% of the time, Pallas kernels for 9%

profile of v1, /device:TPU:1, one launch (start us, length us, event | category | flops | bytes accessed | tf_op | source)
XLA Modules:
  0.0 272.7 jit_solution(6801514738516498117)
XLA Ops:
  1.5 3.3 %collective-permute-start.9 = (f32[2,64,128]{2,1,0:T(8,128)S(1)}, f32[2,64,128]{2,1,0:T(8,128)S(1)}, u32[]{:S(2)}, u32[]{:S(2)}) collective-permute-start(f32[2,64,128]{2,1,0:T(8,128)S(1)} %bitcast_bitcast_fusion), channel_id=1, source_target_pairs={{0,3},{1,2},{2,1},{3,0},{4,7},{5,6},{6,5},{7,4},{8,11},{9,10},{10,... | collective-permute-start | bytes 196616 | tf_op jit(solution)/shard_map/ppermute | solution.py:296
  6.8 2.7 collective-permute-done.8
  9.5 2.8 %collective-permute-start.12 = (f32[8,64,128]{2,1,0:T(8,128)S(1)}, f32[8,64,128]{2,1,0:T(8,128)S(1)}, u32[]{:S(2)}, u32[]{:S(2)}) collective-permute-start(f32[8,64,128]{2,1,0:T(8,128)S(1)} %pad_maximum_fusion), channel_id=1, source_target_pairs={{0,192},{32,224},{64,128},{96,160},{128,64},{160,96},{192,0},{224,... | collective-permute-start | bytes 786440 | tf_op jit(solution)/shard_map/ppermute | solution.py:296
  13.0 9.5 %collective-permute-done.10 = f32[8,64,128]{2,1,0:T(8,128)S(1)} collective-permute-done((f32[8,64,128]{2,1,0:T(8,128)S(1)}, f32[8,64,128]{2,1,0:T(8,128)S(1)}, u32[]{:S(2)}, u32[]{:S(2)}) %collective-permute-start.10) | collective-permute-done | bytes 262176 | tf_op jit(solution)/shard_map/ppermute | solution.py:296
  22.6 0.9 collective-permute-done.12
  23.5 2.6 collective-permute-start.13
  26.0 1.0 copy-done
  27.7 1.4 collective-permute-start.2
  29.0 0.9 collective-permute-start.1
  29.9 1.1 collective-permute-start
  31.7 1.6 collective-permute-done.1
  33.3 2.7 collective-permute-start.5
  37.4 2.9 %collective-permute-done.4 = f32[64,64]{1,0:T(8,128)S(1)} collective-permute-done((f32[64,64]{1,0:T(8,128)S(1)}, f32[64,64]{1,0:T(8,128)S(1)}, u32[]{:S(2)}, u32[]{:S(2)}) %collective-permute-start.4) | collective-permute-done | bytes 16416 | tf_op jit(solution)/shard_map/ppermute | solution.py:296
  40.3 3.0 %collective-permute-start.6 = (f32[64,64]{1,0:T(8,128)S(1)}, f32[64,64]{1,0:T(8,128)S(1)}, u32[]{:S(2)}, u32[]{:S(2)}) collective-permute-start(f32[64,64]{1,0:T(8,128)S(1)} %add_add_fusion.4), channel_id=1, source_target_pairs={{0,32},{32,0},{64,96},{96,64},{128,160},{160,128},{192,224},{224,1... | collective-permute-start | bytes 49160 | tf_op jit(solution)/shard_map/ppermute | solution.py:296
  44.1 5.5 %shard_map.105 = (f32[64,64]{1,0:T(8,128)S(1)}, f32[64,64]{1,0:T(8,128)S(1)}) custom-call(f32[64,64]{1,0:T(8,128)S(1)} %add.116.gram_ref), custom_call_target="tpu_custom_call" | custom-call | tf_op jit(solution)/shard_map/pallas_call | solution.py:285
  49.7 1.0 copy-done.5
  50.7 1.0 copy-done.3
  51.8 1.2 copy-done.6
  55.0 15.9 %shard_map.106 = (f32[64,64,128]{2,1,0:T(8,128)S(1)}, f32[8,2,64,128]{3,2,1,0:T(8,128)S(1)}) custom-call(s32[16]{0:T(128)S(1)} %bitcast.38, s32[16]{0:T(128)S(1)} %fusion.1.near_cols_ref, s32[256]{0:T(256)S(1)} %bitcast.34, s32[256]{0:T(256)S(1)} %bitcast.36, s32[256]{0:T(256)S(1)} %fusion.cols_ref, f32[64,64]{1,0:T(8,128)S(1)} %get-tuple-element.18.refs_0_.base_ref, ...), custom_call_target="tpu_custom_call" | custom-call | tf_op jit(solution)/shard_map/pallas_call | solution.py:264
  71.7 8.2 %all-to-all-start = ((f32[8,2,64,128]{3,2,1,0:T(8,128)}), f32[8,2,64,128]{3,2,1,0:T(8,128)S(1)}, u32[]{:S(2)}, u32[]{:S(2)}) async-start(f32[8,2,64,128]{3,2,1,0:T(8,128)} %copy-done.7), calls=%async_computation | async-start | bytes 1048576 | tf_op jit(solution)/shard_map/all_to_all | solution.py:367
  79.9 17.9 %all-to-all-done.refs_1_ = f32[8,2,64,128]{3,2,1,0:T(8,128)S(1)} async-done(((f32[8,2,64,128]{3,2,1,0:T(8,128)}), f32[8,2,64,128]{3,2,1,0:T(8,128)S(1)}, u32[]{:S(2)}, u32[]{:S(2)}) %all-to-all-start) | async-done | bytes 524320 | tf_op jit(solution)/shard_map/all_to_all | solution.py:367
  98.2 1.7 collective-permute-start.23
  99.9 0.9 collective-permute-start.22
  102.3 1.9 collective-permute-done.21
  106.1 2.2 collective-permute-start.25
  108.2 1.7 collective-permute-start.26
  109.9 1.9 collective-permute-done.24
  112.5 5.6 %collective-permute-done.25 = f32[8,64,128]{2,1,0:T(8,128)S(1)} collective-permute-done((f32[8,64,128]{2,1,0:T(8,128)S(1)}, f32[8,64,128]{2,1,0:T(8,128)S(1)}, u32[]{:S(2)}, u32[]{:S(2)}) %collective-permute-start.25) | collective-permute-done | bytes 262176 | tf_op jit(solution)/shard_map/ppermute | solution.py:296
  118.9 2.8 %collective-permute-done.26 = f32[8,64,128]{2,1,0:T(8,128)S(1)} collective-permute-done((f32[8,64,128]{2,1,0:T(8,128)S(1)}, f32[8,64,128]{2,1,0:T(8,128)S(1)}, u32[]{:S(2)}, u32[]{:S(2)}) %collective-permute-start.26) | collective-permute-done | bytes 262176 | tf_op jit(solution)/shard_map/ppermute | solution.py:296
  122.3 2.2 collective-permute-start.27
  124.5 1.8 collective-permute-start.16
  126.4 1.2 collective-permute-start.15
  127.8 1.7 collective-permute-done.16
  129.4 1.5 collective-permute-done.15
  131.0 1.7 collective-permute-start.19
  132.7 1.6 collective-permute-start.17
  134.3 1.1 collective-permute-done.19
  135.4 2.0 collective-permute-done.18
  137.4 3.3 %collective-permute-start.20 = (f32[128,64]{1,0:T(8,128)S(1)}, f32[128,64]{1,0:T(8,128)S(1)}, u32[]{:S(2)}, u32[]{:S(2)}) collective-permute-start(f32[128,64]{1,0:T(8,128)S(1)} %add_add_fusion.2), channel_id=1, source_target_pairs={{0,32},{32,0},{64,96},{96,64},{128,160},{160,128},{192,224},{224,1... | collective-permute-start | bytes 98312 | tf_op jit(solution)/shard_map/ppermute | solution.py:296
  140.7 0.9 collective-permute-done.20
  142.4 4.1 %all-to-all-start.1 = ((f32[8,128,64]{1,2,0:T(8,128)}), f32[8,128,64]{1,2,0:T(8,128)}, u32[]{:S(2)}, u32[]{:S(2)}) async-start(f32[8,128,64]{1,2,0:T(8,128)} %broadcast_in_dim.6), calls=%async_computation.1 | async-start | bytes 524288 | tf_op jit(solution)/shard_map/all_to_all | solution.py:318
  146.5 1.7 fusion.2
  148.2 10.7 %all-to-all-done.1 = f32[8,128,64]{1,2,0:T(8,128)} async-done(((f32[8,128,64]{1,2,0:T(8,128)}), f32[8,128,64]{1,2,0:T(8,128)}, u32[]{:S(2)}, u32[]{:S(2)}) %all-to-all-start.1) | async-done | bytes 262176 | tf_op jit(solution)/shard_map/all_to_all | solution.py:318
  158.8 1.1 copy.14.grams_ref
  160.0 5.9 %shard_map.108 = (f32[64,64]{1,0:T(8,128)S(1)}, f32[64,64]{1,0:T(8,128)S(1)}, f32[64,64]{1,0:T(8,128)S(1)}, f32[64,64]{1,0:T(8,128)S(1)}) custom-call(f32[8,128,64]{2,1,0:T(8,128)S(1)} %copy.14.grams_ref), custom_call_target="tpu_custom_call" | custom-call | tf_op jit(solution)/shard_map/pallas_call | solution.py:285
  165.9 23.0 %shard_map.109 = (f32[2,64,128]{2,1,0:T(8,128)S(1)}, f32[8,2,64,128]{3,2,1,0:T(8,128)S(1)}) custom-call(s32[16]{0:T(128)S(1)} %bitcast.39, s32[16]{0:T(128)S(1)} %fusion.1.near_cols_ref, s32[256]{0:T(256)S(1)} %bitcast.35, s32[256]{0:T(256)S(1)} %bitcast.37, s32[256]{0:T(256)S(1)} %fusion.cols_ref, f32[64,64]{1,0:T(8,128)S(1)} %get-tuple-element.22.refs_0_.own_ref, ...), custom_call_target="tpu_custom_call" | custom-call | tf_op jit(solution)/shard_map/pallas_call | solution.py:264
  188.9 20.4 %all_to_all.25.refs_2_ = f32[8,2,64,128]{3,2,1,0:T(8,128)S(1)} all-to-all(f32[8,2,64,128]{3,2,1,0:T(8,128)S(1)} %get-tuple-element.26), channel_id=1, replica_groups=mesh['rows'=8,'cols'=8,'seg'=4] {'cols'}, dimensions={0} | all-to-all | bytes 1048576 | tf_op jit(solution)/shard_map/all_to_all | solution.py:380
  210.0 1.4 collective-permute-start.30
  211.4 1.4 collective-permute-start.29
  213.4 1.7 collective-permute-done.30
  215.1 1.4 collective-permute-done.29
  216.5 1.1 collective-permute-done.28
  217.6 1.2 collective-permute-start.33
  218.7 1.1 collective-permute-start.32
  219.8 1.1 collective-permute-start.31
  220.9 1.4 collective-permute-done.33
  222.3 1.4 collective-permute-done.32
  224.3 2.9 %collective-permute-start.34 = (f32[192,64]{1,0:T(8,128)S(1)}, f32[192,64]{1,0:T(8,128)S(1)}, u32[]{:S(2)}, u32[]{:S(2)}) collective-permute-start(f32[192,64]{1,0:T(8,128)S(1)} %add_add_fusion), channel_id=1, source_target_pairs={{0,32},{32,0},{64,96},{96,64},{128,160},{160,128},{192,224},{224,1... | collective-permute-start | bytes 147464 | tf_op jit(solution)/shard_map/ppermute | solution.py:296
  227.2 0.9 collective-permute-done.34
  228.3 20.4 %all_to_all.26 = f32[8,192,64]{1,2,0:T(8,128)S(1)} all-to-all(f32[8,192,64]{1,2,0:T(8,128)S(1)} %broadcast_in_dim.7), channel_id=1, replica_groups=mesh['rows'=8,'cols'=8,'seg'=4] {'cols'}, dimensions={0} | all-to-all | bytes 786432 | tf_op jit(solution)/shard_map/all_to_all | solution.py:318
  249.5 3.5 %all-to-all-start.4 = ((f32[8,2,64,128]{3,2,1,0:T(8,128)}), f32[8,2,64,128]{3,2,1,0:T(8,128)S(1)}, u32[]{:S(2)}, u32[]{:S(2)}) async-start(f32[8,2,64,128]{3,2,1,0:T(8,128)} %broadcast_in_dim.8), calls=%async_computation.4 | async-start | bytes 1048576 | tf_op jit(solution)/shard_map/all_to_all | solution.py:318
  253.3 13.6 %shard_map.111 = (f32[192,128]{1,0:T(8,128)}, f32[64,64]{1,0:T(8,128)S(1)}, f32[64,64]{1,0:T(8,128)S(1)}) custom-call(f32[8,192,64]{2,1,0:T(8,128)S(1)} %copy.16.grams_ref, f32[64,64]{1,0:T(8,128)S(1)} %get-tuple-element.28.start_ref, f32[64,64]{1,0:T(8,128)S(1)} %get-tuple-element.29.head_ref, f32[64,64]{1,0:T(8,128)S(1)} %get-tuple-element.30.lower_ref, ...), custom_call_target="tpu_custom_call" | custom-call | tf_op jit(solution)/shard_map/pallas_call | solution.py:285
  266.9 4.0 %all-to-all-done.4.image_ref = f32[8,2,64,128]{3,2,1,0:T(8,128)S(1)} async-done(((f32[8,2,64,128]{3,2,1,0:T(8,128)}), f32[8,2,64,128]{3,2,1,0:T(8,128)S(1)}, u32[]{:S(2)}, u32[]{:S(2)}) %all-to-all-start.4) | async-done | bytes 524320 | tf_op jit(solution)/shard_map/all_to_all | solution.py:318
  270.9 1.8 shard_map.112
  (87 shorter events, 20.0 us)
Async XLA Ops:
  1.5 5.3 %collective-permute-start.9 = (f32[2,64,128]{2,1,0:T(8,128)S(1)}, f32[2,64,128]{2,1,0:T(8,128)S(1)}, u32[]{:S(2)}, u32[]{:S(2)}) collective-permute-start(f32[2,64,128]{2,1,0:T(8,128)S(1)} %bitcast_bitcast_fusion), channel_id=1, source_target_pairs={{0,3},{1,2},{2,1},{3,0},{4,7},{5,6},{6,5},{7,4},{8,11},{9,10},{10,... | collective-permute-start | bytes 196616 | tf_op jit(solution)/shard_map/ppermute | solution.py:296
  4.8 4.7 %collective-permute-start.8 = (f32[2,64,128]{2,1,0:T(8,128)S(1)}, f32[2,64,128]{2,1,0:T(8,128)S(1)}, u32[]{:S(2)}, u32[]{:S(2)}) collective-permute-start(f32[2,64,128]{2,1,0:T(8,128)S(1)} %bitcast_bitcast_fusion), channel_id=1, source_target_pairs={{0,2},{1,3},{2,0},{3,1},{4,6},{5,7},{6,4},{7,5},{8,10},{9,11},{10,... | collective-permute-start | bytes 196616 | tf_op jit(solution)/shard_map/ppermute | solution.py:296
  5.3 4.2 %collective-permute-start.7 = (f32[2,64,128]{2,1,0:T(8,128)S(1)}, f32[2,64,128]{2,1,0:T(8,128)S(1)}, u32[]{:S(2)}, u32[]{:S(2)}) collective-permute-start(f32[2,64,128]{2,1,0:T(8,128)S(1)} %bitcast_bitcast_fusion), channel_id=1, source_target_pairs={{0,1},{1,0},{2,3},{3,2},{4,5},{5,4},{6,7},{7,6},{8,9},{9,8},{10,11... | collective-permute-start | bytes 196616 | tf_op jit(solution)/shard_map/ppermute | solution.py:296
  9.5 13.9 %collective-permute-start.12 = (f32[8,64,128]{2,1,0:T(8,128)S(1)}, f32[8,64,128]{2,1,0:T(8,128)S(1)}, u32[]{:S(2)}, u32[]{:S(2)}) collective-permute-start(f32[8,64,128]{2,1,0:T(8,128)S(1)} %pad_maximum_fusion), channel_id=1, source_target_pairs={{0,192},{32,224},{64,128},{96,160},{128,64},{160,96},{192,0},{224,... | collective-permute-start | bytes 786440 | tf_op jit(solution)/shard_map/ppermute | solution.py:296
  12.3 10.3 %collective-permute-start.11 = (f32[8,64,128]{2,1,0:T(8,128)S(1)}, f32[8,64,128]{2,1,0:T(8,128)S(1)}, u32[]{:S(2)}, u32[]{:S(2)}) collective-permute-start(f32[8,64,128]{2,1,0:T(8,128)S(1)} %pad_maximum_fusion), channel_id=1, source_target_pairs={{0,128},{32,160},{64,192},{96,224},{128,0},{160,32},{192,64},{224,... | collective-permute-start | bytes 786440 | tf_op jit(solution)/shard_map/ppermute | solution.py:296
  12.6 9.9 %collective-permute-start.10 = (f32[8,64,128]{2,1,0:T(8,128)S(1)}, f32[8,64,128]{2,1,0:T(8,128)S(1)}, u32[]{:S(2)}, u32[]{:S(2)}) collective-permute-start(f32[8,64,128]{2,1,0:T(8,128)S(1)} %pad_maximum_fusion), channel_id=1, source_target_pairs={{0,64},{32,96},{64,0},{96,32},{128,192},{160,224},{192,128},{224,1... | collective-permute-start | bytes 786440 | tf_op jit(solution)/shard_map/ppermute | solution.py:296
  23.5 26.2 %collective-permute-start.13 = (f32[32,64,128]{2,1,0:T(8,128)S(1)}, f32[32,64,128]{2,1,0:T(8,128)S(1)}, u32[]{:S(2)}, u32[]{:S(2)}) collective-permute-start(f32[32,64,128]{2,1,0:T(8,128)S(1)} %constant_dynamic-update-slice_fusion.refs_1_), channel_id=1, source_target_pairs={{0,32},{32,0},{64,96},{96,64},{128,160},{160,128},{192,224},{224,1... | collective-permute-start | bytes 3145736 | tf_op jit(solution)/shard_map/ppermute | solution.py:296
  26.0 1.0 copy-start
  27.7 4.1 %collective-permute-start.2 = (f32[64,64]{1,0:T(8,128)S(1)}, f32[64,64]{1,0:T(8,128)S(1)}, u32[]{:S(2)}, u32[]{:S(2)}) collective-permute-start(f32[64,64]{1,0:T(8,128)S(1)} %shard_map.104), channel_id=1, source_target_pairs={{0,3},{1,2},{2,1},{3,0},{4,7},{5,6},{6,5},{7,4},{8,11},{9,10},{10,... | collective-permute-start | bytes 49160 | tf_op jit(solution)/shard_map/ppermute | solution.py:296
  29.0 4.3 %collective-permute-start.1 = (f32[64,64]{1,0:T(8,128)S(1)}, f32[64,64]{1,0:T(8,128)S(1)}, u32[]{:S(2)}, u32[]{:S(2)}) collective-permute-start(f32[64,64]{1,0:T(8,128)S(1)} %shard_map.104), channel_id=1, source_target_pairs={{0,2},{1,3},{2,0},{3,1},{4,6},{5,7},{6,4},{7,5},{8,10},{9,11},{10,... | collective-permute-start | bytes 49160 | tf_op jit(solution)/shard_map/ppermute | solution.py:296
  29.9 3.4 %collective-permute-start = (f32[64,64]{1,0:T(8,128)S(1)}, f32[64,64]{1,0:T(8,128)S(1)}, u32[]{:S(2)}, u32[]{:S(2)}) collective-permute-start(f32[64,64]{1,0:T(8,128)S(1)} %shard_map.104), channel_id=1, source_target_pairs={{0,1},{1,0},{2,3},{3,2},{4,5},{5,4},{6,7},{7,6},{8,9},{9,8},{10,11... | collective-permute-start | bytes 49160 | tf_op jit(solution)/shard_map/ppermute | solution.py:296
  33.3 4.1 %collective-permute-start.5 = (f32[64,64]{1,0:T(8,128)S(1)}, f32[64,64]{1,0:T(8,128)S(1)}, u32[]{:S(2)}, u32[]{:S(2)}) collective-permute-start(f32[64,64]{1,0:T(8,128)S(1)} %add_add_fusion.5), channel_id=1, source_target_pairs={{0,192},{32,224},{64,128},{96,160},{128,64},{160,96},{192,0},{224,... | collective-permute-start | bytes 49160 | tf_op jit(solution)/shard_map/ppermute | solution.py:296
  36.0 4.3 %collective-permute-start.4 = (f32[64,64]{1,0:T(8,128)S(1)}, f32[64,64]{1,0:T(8,128)S(1)}, u32[]{:S(2)}, u32[]{:S(2)}) collective-permute-start(f32[64,64]{1,0:T(8,128)S(1)} %add_add_fusion.5), channel_id=1, source_target_pairs={{0,128},{32,160},{64,192},{96,224},{128,0},{160,32},{192,64},{224,... | collective-permute-start | bytes 49160 | tf_op jit(solution)/shard_map/ppermute | solution.py:296
  36.3 3.9 %collective-permute-start.3 = (f32[64,64]{1,0:T(8,128)S(1)}, f32[64,64]{1,0:T(8,128)S(1)}, u32[]{:S(2)}, u32[]{:S(2)}) collective-permute-start(f32[64,64]{1,0:T(8,128)S(1)} %add_add_fusion.5), channel_id=1, source_target_pairs={{0,64},{32,96},{64,0},{96,32},{128,192},{160,224},{192,128},{224,1... | collective-permute-start | bytes 49160 | tf_op jit(solution)/shard_map/ppermute | solution.py:296
  40.3 3.9 %collective-permute-start.6 = (f32[64,64]{1,0:T(8,128)S(1)}, f32[64,64]{1,0:T(8,128)S(1)}, u32[]{:S(2)}, u32[]{:S(2)}) collective-permute-start(f32[64,64]{1,0:T(8,128)S(1)} %add_add_fusion.4), channel_id=1, source_target_pairs={{0,32},{32,0},{64,96},{96,64},{128,160},{160,128},{192,224},{224,1... | collective-permute-start | bytes 49160 | tf_op jit(solution)/shard_map/ppermute | solution.py:296
  49.7 1.0 copy-start.5
  50.7 1.0 copy-start.3
  51.8 1.2 copy-start.6
  53.0 0.7 copy-start.8
  53.7 0.7 copy-start.10
  54.3 0.7 copy-start.12
  70.9 0.8 copy-start.7
  71.7 70.7 %copy-start.2 = (f32[64,64,128]{2,1,0:T(8,128)}, f32[64,64,128]{2,1,0:T(8,128)S(1)}, u32[]{:S(2)}) copy-start(f32[64,64,128]{2,1,0:T(8,128)S(1)} %get-tuple-element.19) | copy-start | bytes 6291460
  71.7 26.2 %all-to-all-start = ((f32[8,2,64,128]{3,2,1,0:T(8,128)}), f32[8,2,64,128]{3,2,1,0:T(8,128)S(1)}, u32[]{:S(2)}, u32[]{:S(2)}) async-start(f32[8,2,64,128]{3,2,1,0:T(8,128)} %copy-done.7), calls=%async_computation | async-start | bytes 1048576 | tf_op jit(solution)/shard_map/all_to_all | solution.py:367
  98.2 7.2 %collective-permute-start.23 = (f32[2,64,128]{2,1,0:T(8,128)S(1)}, f32[2,64,128]{2,1,0:T(8,128)S(1)}, u32[]{:S(2)}, u32[]{:S(2)}) collective-permute-start(f32[2,64,128]{2,1,0:T(8,128)S(1)} %get-tuple-element.24), channel_id=1, source_target_pairs={{0,3},{1,2},{2,1},{3,0},{4,7},{5,6},{6,5},{7,4},{8,11},{9,10},{10,... | collective-permute-start | bytes 196616 | tf_op jit(solution)/shard_map/ppermute | solution.py:296
  99.9 4.9 %collective-permute-start.22 = (f32[2,64,128]{2,1,0:T(8,128)S(1)}, f32[2,64,128]{2,1,0:T(8,128)S(1)}, u32[]{:S(2)}, u32[]{:S(2)}) collective-permute-start(f32[2,64,128]{2,1,0:T(8,128)S(1)} %get-tuple-element.24), channel_id=1, source_target_pairs={{0,2},{1,3},{2,0},{3,1},{4,6},{5,7},{6,4},{7,5},{8,10},{9,11},{10,... | collective-permute-start | bytes 196616 | tf_op jit(solution)/shard_map/ppermute | solution.py:296
  100.9 3.3 %collective-permute-start.21 = (f32[2,64,128]{2,1,0:T(8,128)S(1)}, f32[2,64,128]{2,1,0:T(8,128)S(1)}, u32[]{:S(2)}, u32[]{:S(2)}) collective-permute-start(f32[2,64,128]{2,1,0:T(8,128)S(1)} %get-tuple-element.24), channel_id=1, source_target_pairs={{0,1},{1,0},{2,3},{3,2},{4,5},{5,4},{6,7},{7,6},{8,9},{9,8},{10,11... | collective-permute-start | bytes 196616 | tf_op jit(solution)/shard_map/ppermute | solution.py:296
  106.0 5.8 %collective-permute-start.24 = (f32[8,64,128]{2,1,0:T(8,128)S(1)}, f32[8,64,128]{2,1,0:T(8,128)S(1)}, u32[]{:S(2)}, u32[]{:S(2)}) collective-permute-start(f32[8,64,128]{2,1,0:T(8,128)S(1)} %get-tuple-element.36), channel_id=1, source_target_pairs={{0,64},{32,96},{64,0},{96,32},{128,192},{160,224},{192,128},{224,1... | collective-permute-start | bytes 786440 | tf_op jit(solution)/shard_map/ppermute | solution.py:296
  106.1 12.1 %collective-permute-start.25 = (f32[8,64,128]{2,1,0:T(8,128)S(1)}, f32[8,64,128]{2,1,0:T(8,128)S(1)}, u32[]{:S(2)}, u32[]{:S(2)}) collective-permute-start(f32[8,64,128]{2,1,0:T(8,128)S(1)} %get-tuple-element.36), channel_id=1, source_target_pairs={{0,128},{32,160},{64,192},{96,224},{128,0},{160,32},{192,64},{224,... | collective-permute-start | bytes 786440 | tf_op jit(solution)/shard_map/ppermute | solution.py:296
  108.2 13.4 %collective-permute-start.26 = (f32[8,64,128]{2,1,0:T(8,128)S(1)}, f32[8,64,128]{2,1,0:T(8,128)S(1)}, u32[]{:S(2)}, u32[]{:S(2)}) collective-permute-start(f32[8,64,128]{2,1,0:T(8,128)S(1)} %get-tuple-element.36), channel_id=1, source_target_pairs={{0,192},{32,224},{64,128},{96,160},{128,64},{160,96},{192,0},{224,... | collective-permute-start | bytes 786440 | tf_op jit(solution)/shard_map/ppermute | solution.py:296
  112.5 53.3 %copy-start.4 = (bf16[1,1,1,16,128,128]{5,4,3,2,1,0:T(8,128)(2,1)S(1)}, bf16[1,1,1,16,128,128]{5,4,3,2,1,0:T(8,128)(2,1)}, u32[]{:S(2)}) copy-start(bf16[1,1,1,16,128,128]{5,4,3,2,1,0:T(8,128)(2,1)} %param.10) | copy-start | bytes 1572868
  112.5 53.4 %copy-start.9 = (s32[1,1,1,256]{3,2,1,0:T(1,128)S(1)}, s32[1,1,1,256]{3,2,1,0:T(1,128)}, u32[]{:S(2)}) copy-start(s32[1,1,1,256]{3,2,1,0:T(1,128)} %param.15) | copy-start | bytes 3076
  112.5 53.4 %copy-start.11 = (s32[1,1,1,256]{3,2,1,0:T(1,128)S(1)}, s32[1,1,1,256]{3,2,1,0:T(1,128)}, u32[]{:S(2)}) copy-start(s32[1,1,1,256]{3,2,1,0:T(1,128)} %param.16) | copy-start | bytes 3076
  112.5 53.4 %copy-start.13 = (s32[1,1,1,16]{3,2,1,0:T(1,128)S(1)}, s32[1,1,1,16]{3,2,1,0:T(1,128)}, u32[]{:S(2)}) copy-start(s32[1,1,1,16]{3,2,1,0:T(1,128)} %param.11) | copy-start | bytes 196
  122.3 43.5 %collective-permute-start.27 = (f32[32,64,128]{2,1,0:T(8,128)}, f32[32,64,128]{2,1,0:T(8,128)}, u32[]{:S(2)}, u32[]{:S(2)}) collective-permute-start(f32[32,64,128]{2,1,0:T(8,128)} %constant_dynamic-update-slice_fusion.11.refs_2_), channel_id=1, source_target_pairs={{0,32},{32,0},{64,96},{96,64},{128,160},{160,128},{192,224},{224,1... | collective-permute-start | bytes 3145736 | tf_op jit(solution)/shard_map/ppermute | solution.py:296
  124.5 4.9 %collective-permute-start.16 = (f32[128,64]{1,0:T(8,128)S(1)}, f32[128,64]{1,0:T(8,128)S(1)}, u32[]{:S(2)}, u32[]{:S(2)}) collective-permute-start(f32[128,64]{1,0:T(8,128)S(1)} %get-tuple-element.21), channel_id=1, source_target_pairs={{0,3},{1,2},{2,1},{3,0},{4,7},{5,6},{6,5},{7,4},{8,11},{9,10},{10,... | collective-permute-start | bytes 98312 | tf_op jit(solution)/shard_map/ppermute | solution.py:296
  126.4 4.6 %collective-permute-start.15 = (f32[128,64]{1,0:T(8,128)S(1)}, f32[128,64]{1,0:T(8,128)S(1)}, u32[]{:S(2)}, u32[]{:S(2)}) collective-permute-start(f32[128,64]{1,0:T(8,128)S(1)} %get-tuple-element.21), channel_id=1, source_target_pairs={{0,2},{1,3},{2,0},{3,1},{4,6},{5,7},{6,4},{7,5},{8,10},{9,11},{10,... | collective-permute-start | bytes 98312 | tf_op jit(solution)/shard_map/ppermute | solution.py:296
  127.6 3.4 %collective-permute-start.14 = (f32[128,64]{1,0:T(8,128)S(1)}, f32[128,64]{1,0:T(8,128)S(1)}, u32[]{:S(2)}, u32[]{:S(2)}) collective-permute-start(f32[128,64]{1,0:T(8,128)S(1)} %get-tuple-element.21), channel_id=1, source_target_pairs={{0,1},{1,0},{2,3},{3,2},{4,5},{5,4},{6,7},{7,6},{8,9},{9,8},{10,11... | collective-permute-start | bytes 98312 | tf_op jit(solution)/shard_map/ppermute | solution.py:296
  131.0 4.4 %collective-permute-start.19 = (f32[128,64]{1,0:T(8,128)S(1)}, f32[128,64]{1,0:T(8,128)S(1)}, u32[]{:S(2)}, u32[]{:S(2)}) collective-permute-start(f32[128,64]{1,0:T(8,128)S(1)} %add_add_fusion.3), channel_id=1, source_target_pairs={{0,192},{32,224},{64,128},{96,160},{128,64},{160,96},{192,0},{224,... | collective-permute-start | bytes 98312 | tf_op jit(solution)/shard_map/ppermute | solution.py:296
  132.7 4.7 %collective-permute-start.18 = (f32[128,64]{1,0:T(8,128)S(1)}, f32[128,64]{1,0:T(8,128)S(1)}, u32[]{:S(2)}, u32[]{:S(2)}) collective-permute-start(f32[128,64]{1,0:T(8,128)S(1)} %add_add_fusion.3), channel_id=1, source_target_pairs={{0,128},{32,160},{64,192},{96,224},{128,0},{160,32},{192,64},{224,... | collective-permute-start | bytes 98312 | tf_op jit(solution)/shard_map/ppermute | solution.py:296
  132.7 4.7 %collective-permute-start.17 = (f32[128,64]{1,0:T(8,128)S(1)}, f32[128,64]{1,0:T(8,128)S(1)}, u32[]{:S(2)}, u32[]{:S(2)}) collective-permute-start(f32[128,64]{1,0:T(8,128)S(1)} %add_add_fusion.3), channel_id=1, source_target_pairs={{0,64},{32,96},{64,0},{96,32},{128,192},{160,224},{192,128},{224,1... | collective-permute-start | bytes 98312 | tf_op jit(solution)/shard_map/ppermute | solution.py:296
  137.4 4.2 %collective-permute-start.20 = (f32[128,64]{1,0:T(8,128)S(1)}, f32[128,64]{1,0:T(8,128)S(1)}, u32[]{:S(2)}, u32[]{:S(2)}) collective-permute-start(f32[128,64]{1,0:T(8,128)S(1)} %add_add_fusion.2), channel_id=1, source_target_pairs={{0,32},{32,0},{64,96},{96,64},{128,160},{160,128},{192,224},{224,1... | collective-permute-start | bytes 98312 | tf_op jit(solution)/shard_map/ppermute | solution.py:296
  142.4 16.4 %all-to-all-start.1 = ((f32[8,128,64]{1,2,0:T(8,128)}), f32[8,128,64]{1,2,0:T(8,128)}, u32[]{:S(2)}, u32[]{:S(2)}) async-start(f32[8,128,64]{1,2,0:T(8,128)} %broadcast_in_dim.6), calls=%async_computation.1 | async-start | bytes 524288 | tf_op jit(solution)/shard_map/all_to_all | solution.py:318
  188.9 82.0 %copy-start.1 = (f32[64,2048]{1,0:T(8,128)S(1)}, f32[64,2048]{1,0:T(8,128)}, u32[]{:S(2)}) copy-start(f32[64,2048]{1,0:T(8,128)} %right_ref.1) | copy-start | bytes 1572868
  210.0 5.1 %collective-permute-start.30 = (f32[192,64]{1,0:T(8,128)S(1)}, f32[192,64]{1,0:T(8,128)S(1)}, u32[]{:S(2)}, u32[]{:S(2)}) collective-permute-start(f32[192,64]{1,0:T(8,128)S(1)} %get-tuple-element.27), channel_id=1, source_target_pairs={{0,3},{1,2},{2,1},{3,0},{4,7},{5,6},{6,5},{7,4},{8,11},{9,10},{10,... | collective-permute-start | bytes 147464 | tf_op jit(solution)/shard_map/ppermute | solution.py:296
  211.4 5.1 %collective-permute-start.29 = (f32[192,64]{1,0:T(8,128)S(1)}, f32[192,64]{1,0:T(8,128)S(1)}, u32[]{:S(2)}, u32[]{:S(2)}) collective-permute-start(f32[192,64]{1,0:T(8,128)S(1)} %get-tuple-element.27), channel_id=1, source_target_pairs={{0,2},{1,3},{2,0},{3,1},{4,6},{5,7},{6,4},{7,5},{8,10},{9,11},{10,... | collective-permute-start | bytes 147464 | tf_op jit(solution)/shard_map/ppermute | solution.py:296
  212.7 4.8 %collective-permute-start.28 = (f32[192,64]{1,0:T(8,128)S(1)}, f32[192,64]{1,0:T(8,128)S(1)}, u32[]{:S(2)}, u32[]{:S(2)}) collective-permute-start(f32[192,64]{1,0:T(8,128)S(1)} %get-tuple-element.27), channel_id=1, source_target_pairs={{0,1},{1,0},{2,3},{3,2},{4,5},{5,4},{6,7},{7,6},{8,9},{9,8},{10,11... | collective-permute-start | bytes 147464 | tf_op jit(solution)/shard_map/ppermute | solution.py:296
  217.6 4.8 %collective-permute-start.33 = (f32[192,64]{1,0:T(8,128)S(1)}, f32[192,64]{1,0:T(8,128)S(1)}, u32[]{:S(2)}, u32[]{:S(2)}) collective-permute-start(f32[192,64]{1,0:T(8,128)S(1)} %add_add_fusion.1), channel_id=1, source_target_pairs={{0,192},{32,224},{64,128},{96,160},{128,64},{160,96},{192,0},{224,... | collective-permute-start | bytes 147464 | tf_op jit(solution)/shard_map/ppermute | solution.py:296
  218.7 5.0 %collective-permute-start.32 = (f32[192,64]{1,0:T(8,128)S(1)}, f32[192,64]{1,0:T(8,128)S(1)}, u32[]{:S(2)}, u32[]{:S(2)}) collective-permute-start(f32[192,64]{1,0:T(8,128)S(1)} %add_add_fusion.1), channel_id=1, source_target_pairs={{0,128},{32,160},{64,192},{96,224},{128,0},{160,32},{192,64},{224,... | collective-permute-start | bytes 147464 | tf_op jit(solution)/shard_map/ppermute | solution.py:296
  219.8 4.4 %collective-permute-start.31 = (f32[192,64]{1,0:T(8,128)S(1)}, f32[192,64]{1,0:T(8,128)S(1)}, u32[]{:S(2)}, u32[]{:S(2)}) collective-permute-start(f32[192,64]{1,0:T(8,128)S(1)} %add_add_fusion.1), channel_id=1, source_target_pairs={{0,64},{32,96},{64,0},{96,32},{128,192},{160,224},{192,128},{224,1... | collective-permute-start | bytes 147464 | tf_op jit(solution)/shard_map/ppermute | solution.py:296
  224.3 3.9 %collective-permute-start.34 = (f32[192,64]{1,0:T(8,128)S(1)}, f32[192,64]{1,0:T(8,128)S(1)}, u32[]{:S(2)}, u32[]{:S(2)}) collective-permute-start(f32[192,64]{1,0:T(8,128)S(1)} %add_add_fusion), channel_id=1, source_target_pairs={{0,32},{32,0},{64,96},{96,64},{128,160},{160,128},{192,224},{224,1... | collective-permute-start | bytes 147464 | tf_op jit(solution)/shard_map/ppermute | solution.py:296
  249.5 21.4 %all-to-all-start.4 = ((f32[8,2,64,128]{3,2,1,0:T(8,128)}), f32[8,2,64,128]{3,2,1,0:T(8,128)S(1)}, u32[]{:S(2)}, u32[]{:S(2)}) async-start(f32[8,2,64,128]{3,2,1,0:T(8,128)} %broadcast_in_dim.8), calls=%async_computation.4 | async-start | bytes 1048576 | tf_op jit(solution)/shard_map/all_to_all | solution.py:318

commit v2 on v1

v2 whole, which is shorter than its diff:
```python
import functools

import jax
import jax.numpy as jnp
from jax import lax
from jax.experimental import pallas as pl
from jax.experimental.pallas import tpu as pltpu
from jax.sharding import PartitionSpec as P

FULL = lax.Precision.HIGHEST
NN = (((1,), (0,)), ((), ()))
NT = (((1,), (1,)), ((), ()))
TN = (((0,), (0,)), ((), ()))
CHUNKS = 8
UNROLL = 32
VMEM_LIMIT = 48 * 1024 * 1024


def mm(a, b, dims=NN):
    return lax.dot_general(a, b, dims, precision=FULL, preferred_element_type=jnp.float32)


def vmem():
    return pl.BlockSpec(memory_space=pltpu.VMEM)


def smem():
    return pl.BlockSpec(memory_space=pltpu.SMEM)


def eye(order):
    rows = lax.broadcasted_iota(jnp.int32, (order, order), 0)
    cols = lax.broadcasted_iota(jnp.int32, (order, order), 1)
    return (rows == cols).astype(jnp.float32)


def eliminate(works):
    order = works[0].shape[0]
    groups = [[work[at : at + 8] for at in range(0, order, 8)] for work in works]
    places = lax.broadcasted_iota(jnp.int32, groups[0][0].shape, 0)

    def lane(value, at):
        return jnp.broadcast_to(value[:, at : at + 1], value.shape)

    def pivots(parts, base):
        head = parts[base // 8]
        rows = [jnp.broadcast_to(head[at : at + 1], head.shape) for at in range(8)]
        corner = [[lane(row, base + at) for at in range(8)] for row in rows]
        steps, ratios, scaled = [], [], []
        for at in range(8):
            inverse = 1.0 / corner[at][at]
            ratio = {later: corner[at][later] * inverse for later in range(at + 1, 8)}
            steps.append(rows[at] * inverse)
            ratios.append(ratio)
            scaled.append(rows[at] * (1.0 / jnp.sqrt(corner[at][at])))
            for later in range(at + 1, 8):
                rows[later] = rows[later] - ratio[later] * rows[at]
                for column in range(later, 8):
                    corner[later][column] = corner[later][column] - ratio[later] * corner[at][column]
        result = scaled[0]
        for at in range(1, 8):
            result = jnp.where(places == at, scaled[at], result)
        return result, steps, ratios

    for base in range(0, order, 8):
        for parts in groups:
            parts[base // 8], steps, ratios = pivots(parts, base)
            for below in range(base // 8 + 1, len(parts)):
                value = parts[below]
                factors = [lane(value, base + at) for at in range(8)]
                for at in range(8):
                    for earlier in range(at):
                        factors[at] = factors[at] - ratios[earlier][at] * factors[earlier]
                for at in range(8):
                    value = value - factors[at] * steps[at]
                parts[below] = value
    results = []
    for parts in groups:
        work = jnp.concatenate(parts, 0)
        rows = lax.broadcasted_iota(jnp.int32, work.shape, 0)
        cols = lax.broadcasted_iota(jnp.int32, work.shape, 1)
        results.append(jnp.where(cols >= rows, work, 0.0))
    return results


def split(value):
    high = value.astype(jnp.bfloat16)
    return high, (value - high.astype(jnp.float32)).astype(jnp.bfloat16)


def sum_leading(ref):
    total = ref[0]
    for index in range(1, ref.shape[0]):
        total = total + ref[index].astype(jnp.float32)
    return total


def start_kernel(column_ref, piece_ref, message_ref):
    piece = piece_ref[...]
    group, leaf = message_ref.shape[0] - 1, message_ref.shape[2]
    for half in range(group):
        first = pl.multiple_of((column_ref[0] * group + half) * leaf, leaf)
        message_ref[half] = piece_ref[:, pl.ds(first, leaf)]
    gram = mm(piece, piece, NT)
    message_ref[group] = jnp.concatenate([gram, jnp.zeros_like(gram)], 1)


def share_products(bases, share):
    group = len(share)
    products = []
    for base in bases + [share]:
        total = mm(base[0], share[0], NT)
        for half in range(1, group):
            total = total + mm(base[half], share[half], NT)
        products.append(total)
    return products


def in_cells(ref):
    parts = [ref[at, half] for at in range(ref.shape[0]) for half in range(ref.shape[1])]
    return jnp.concatenate(parts, 1)


def sum_kernel(terms_ref, share_ref):
    share_ref[...] = sum_leading(terms_ref)


def first_image_kernel(base_ref, right_ref, image_ref, share_ref, message_ref):
    basis = mm(base_ref[...], right_ref[...])
    image = in_cells(image_ref)
    order, group = image.shape[0], share_ref.shape[0]
    products = mm(jnp.concatenate([basis, image], 0), image, NT)
    message_ref[:group] = share_ref[...]
    message_ref[group] = jnp.concatenate([products[:order], products[order:]], 1)


def second_image_kernel(first_ref, second_ref, terms_ref, gram_ref):
    total = terms_ref[0].astype(jnp.float32)
    for index in range(1, terms_ref.shape[0]):
        total = total + terms_ref[index].astype(jnp.float32)
    group, order = total.shape[0], total.shape[1]
    share = [total[half] for half in range(group)]
    bases = [[ref[half] for half in range(group)] for ref in (first_ref, second_ref)]
    one, two, square = share_products(bases, share)
    gram_ref[:order] = jnp.concatenate([one, two], 1)
    gram_ref[order:] = jnp.concatenate([square[: order // 2], square[order // 2 :]], 1)


def merge_kernel(own_ref, one_ref, two_ref, three_ref, out_ref):
    refs = (own_ref, one_ref, two_ref, three_ref)
    count = own_ref.shape[0] - 1
    for at, ref in enumerate(refs):
        out_ref[at * count : (at + 1) * count] = ref[:count]
    out_ref[4 * count] = (own_ref[count] + one_ref[count]) + (two_ref[count] + three_ref[count])


def final_kernel(
    grams_ref,
    start_ref,
    head_ref,
    lower_ref,
    top_inverse_ref,
    own_ref,
    mix_ref,
    base_ref,
    right_ref,
    image_ref,
    out_ref,
    hessen_ref,
):
    totals = sum_leading(grams_ref)
    order = start_ref.shape[0]
    unit = eye(order)
    cross_one = totals[:order, :order]
    inner = totals[:order, order:]
    square = jnp.concatenate([totals[order:, :order], totals[order:, order:]], 0)
    cross_two = inner + 0.5 * unit
    gram = square - mm(cross_one, cross_one, TN) - mm(inner, inner, TN)
    start, head, lower = start_ref[...], head_ref[...], lower_ref[...]
    top_inverse = top_inverse_ref[...]
    side = mm(head, cross_one, TN) + mm(lower, cross_two, TN)
    corner = mm(cross_one, cross_one, TN) + mm(cross_two, cross_two, TN) + gram
    bridge = mm(top_inverse, side)
    part = mm(top_inverse, mm(head, start, TN))
    schur = corner - mm(bridge, bridge, TN)
    rest = mm(cross_one, start, TN) - mm(bridge, part, TN)
    schur_done, gram_done = eliminate(
        [jnp.concatenate([schur, unit], 1), jnp.concatenate([gram, rest], 1)]
    )
    low_inverse = schur_done[:, order:]
    low_weights = mm(low_inverse, mm(low_inverse, rest), TN)
    top_weights = mm(top_inverse, part - mm(bridge, low_weights), TN)
    hessen_ref[:order, :] = jnp.concatenate([head, cross_one], 1)
    hessen_ref[order : 2 * order, :] = jnp.concatenate([lower, cross_two], 1)
    hessen_ref[2 * order :, :] = jnp.concatenate([jnp.zeros_like(head), gram_done[:, :order]], 1)
    for_image = mm(low_weights, own_ref[...], TN)
    for_right = mm(top_weights, base_ref[...], TN) + mm(low_weights, mix_ref[...], TN)
    weights = jnp.concatenate([for_right, for_image], 1)
    out_ref[...] = mm(weights, jnp.concatenate([right_ref[...], in_cells(image_ref)], 0))


def start_mixes(gram_refs, out_refs):
    last = gram_refs[0].shape[0] - 1
    totals = gram_refs[0][last] + gram_refs[1][last]
    order = totals.shape[0]
    (done,) = eliminate([jnp.concatenate([totals[:, :order], eye(order)], 1)])
    factor_ref, base_ref = out_refs
    factor_ref[...] = done[:, :order]
    base_ref[...] = done[:, order:]
    return [done[:, order:]]


def middle_mixes(gram_refs, out_refs):
    last = gram_refs[0].shape[0] - 1
    totals = gram_refs[0][last] + gram_refs[1][last]
    base = gram_refs[2][...]
    order = totals.shape[0]
    unit = eye(order)
    cross, square = totals[:, :order], totals[:, order:]
    gram = square - mm(cross, cross, TN)
    head = cross + 0.5 * unit
    top = mm(head, head, TN) + gram
    done, top_done = eliminate(
        [jnp.concatenate([gram, unit], 1), jnp.concatenate([top, unit], 1)]
    )
    own = done[:, order:]
    mix = -mm(mm(own, cross, NT), base)
    head_ref, lower_ref, top_inverse_ref, own_ref, mix_ref = out_refs
    head_ref[...] = head
    lower_ref[...] = done[:, :order]
    top_inverse_ref[...] = top_done[:, order:]
    own_ref[...] = own
    mix_ref[...] = mix
    return [own, mix]


def apply_kernel(prepare, gram_count, out_count, panels, slots_ref, *refs):
    gram_refs, refs = refs[:gram_count], refs[gram_count:]
    panel_refs, refs = refs[: 2 * panels], refs[2 * panels :]
    near_hbm, left_hbm, right_hbm = refs[:3]
    small_outs, refs = refs[3 : 3 + out_count], refs[3 + out_count :]
    basis_ref, terms_ref = refs[:2]
    total, rounded, near, left, right, sems, near_sem = refs[2:]
    slots = left.shape[0]
    per = slots // CHUNKS
    near_copy = pltpu.make_async_copy(near_hbm, near, near_sem)
    near_copy.start()
    copies = []
    for chunk in range(CHUNKS):
        part = pl.ds(chunk * per, per)
        pair = (
            pltpu.make_async_copy(right_hbm.at[part], right.at[part], sems.at[chunk, 0]),
            pltpu.make_async_copy(left_hbm.at[part], left.at[part], sems.at[chunk, 1]),
        )
        for copy in pair:
            copy.start()
        copies.append(pair)
    total[...] = jnp.zeros_like(total)
    mixes = prepare(gram_refs, small_outs)
    group = total.shape[1]
    for half in range(group):
        share = mm(mixes[0], panel_refs[0][half])
        for at in range(1, panels):
            share = share + mm(mixes[at], panel_refs[2 * at][half])
        basis_ref[half] = share
    high, low = split(jnp.concatenate(mixes, 1))
    weights = jnp.concatenate([high, high, low], 1)
    half_count = rounded.shape[0] // 2
    for side in range(2):

        def make_basis(index, _, side=side):
            stacked = jnp.concatenate([panel_refs[2 * at + side][index] for at in range(panels)], 0)
            upper, under = split(stacked)
            value = lax.dot_general(
                weights,
                jnp.concatenate([upper, under, upper], 0),
                NN,
                preferred_element_type=jnp.float32,
            )
            rounded[side * half_count + index] = value.astype(jnp.bfloat16)
            return 0

        lax.fori_loop(0, half_count, make_basis, 0, unroll=8)

    order = rounded.shape[1]
    columns = lax.broadcasted_iota(jnp.int32, (order, left.shape[1]), 1)

    def row_and_column(packed):
        return (packed >> 8) & 255, packed & 255

    near_copy.wait()

    def near_step(step, _):
        values = []
        for inner in range(4):
            at = step * 4 + inner
            row, column = row_and_column(slots_ref[slots + at])
            value = lax.dot_general(rounded[column], near[at], NT, preferred_element_type=jnp.float32)
            values.append((row, value))
        for row, value in values:
            total[row // group, row % group] += value
        return 0

    lax.fori_loop(0, near.shape[0] // 4, near_step, 0)

    def slot_step(step, _):
        coefs = []
        for inner in range(UNROLL):
            at = step * UNROLL + inner
            packed = slots_ref[at]
            row, column = row_and_column(packed)
            coef = lax.dot_general(rounded[column], right[at], NT, preferred_element_type=jnp.float32)
            coef = jnp.where(columns < (packed >> 16), coef, 0.0).astype(jnp.bfloat16)
            coefs.append((row, coef))
        values = []
        for inner, (row, coef) in enumerate(coefs):
            value = lax.dot_general(
                coef, left[step * UNROLL + inner], NN, preferred_element_type=jnp.float32
            )
            values.append((row, value))
        for row, value in values:
            total[row // group, row % group] += value
        return 0

    for chunk in range(CHUNKS):
        for copy in copies[chunk]:
            copy.wait()
        lax.fori_loop(chunk * per // UNROLL, (chunk + 1) * per // UNROLL, slot_step, 0)
    terms_ref[...] = total[...].astype(terms_ref.dtype)


def apply_operator(prepare, small_count, grams, halves, operator, terms_shape, terms_dtype):
    slots, near, left, right = operator
    group, order, leaf = terms_shape[1:]
    clusters = 2 * (halves[0].shape[0] - 1)
    panels = len(halves) // 2
    square = jax.ShapeDtypeStruct((order, order), jnp.float32)
    return pl.pallas_call(
        functools.partial(apply_kernel, prepare, len(grams), small_count, panels),
        out_shape=(
            *[square] * small_count,
            jax.ShapeDtypeStruct((group, order, leaf), jnp.float32),
            jax.ShapeDtypeStruct(terms_shape, terms_dtype),
        ),
        in_specs=[smem()]
        + [vmem()] * (len(grams) + len(halves))
        + [pl.BlockSpec(memory_space=pl.ANY)] * 3,
        out_specs=tuple(vmem() for _ in range(small_count + 2)),
        scratch_shapes=[
            pltpu.VMEM(terms_shape, jnp.float32),
            pltpu.VMEM((clusters, order, leaf), jnp.bfloat16),
            pltpu.VMEM(near.shape, near.dtype),
            pltpu.VMEM(left.shape, left.dtype),
            pltpu.VMEM(right.shape, right.dtype),
            pltpu.SemaphoreType.DMA((CHUNKS, 2)),
            pltpu.SemaphoreType.DMA,
        ],
        compiler_params=pltpu.CompilerParams(vmem_limit_bytes=VMEM_LIMIT),
    )(slots, *grams, *halves, near, left, right)


def call(kernel, outs, *operands, specs=None):
    return pl.pallas_call(
        kernel,
        out_shape=tuple(jax.ShapeDtypeStruct(shape, jnp.float32) for shape in outs),
        in_specs=specs or [vmem()] * len(operands),
        out_specs=tuple(vmem() for _ in outs),
        compiler_params=pltpu.CompilerParams(vmem_limit_bytes=VMEM_LIMIT),
    )(*operands)


def exchange(values, axis, distance):
    count = lax.axis_size(axis)
    return lax.ppermute(values, axis, [(at, at ^ distance) for at in range(count)])


SEG_STEPS = ("seg", (1, 2, 3))
CHIP_STEPS = ("rows", (2, 4, 6))


def reduce_rows_seg(values):
    for axis, steps in (SEG_STEPS, CHIP_STEPS):
        one, two, three = [exchange(values, axis, step) for step in steps]
        values = (values + one) + (two + three)
    return values + exchange(values, "rows", 1)


def gather_halves(message):
    for axis, steps in (SEG_STEPS, CHIP_STEPS):
        merged = (4 * (message.shape[0] - 1) + 1,) + message.shape[1:]
        (message,) = call(merge_kernel, [merged], message, *[exchange(message, axis, step) for step in steps])
    return [message, exchange(message, "rows", 1)]


def spread_cols(values):
    count = lax.axis_size("cols")
    return lax.all_to_all(jnp.broadcast_to(values[None], (count,) + values.shape), "cols", 0, 0)


def body(
    right_side,
    near_blocks,
    near_rows,
    near_cols,
    left_factors,
    right_factors,
    slot_ranks,
    slot_rows,
    slot_cols,
):
    col_count = lax.axis_size("cols")
    col_index = lax.axis_index("cols")
    order, cells = right_side.shape
    leaf = near_blocks.shape[-1]
    group = cells // leaf // col_count
    me = lax.axis_index("rows") * lax.axis_size("seg") + lax.axis_index("seg")

    def packed(ranks, rows, columns):
        piece = (columns // group) ^ me
        place = ((piece >> 3) & 3) * 4 + ((piece >> 2) & 1) * 16 + (piece & 3)
        return ranks * 65536 + rows * 256 + place * group + columns % group

    operator = (
        jnp.concatenate(
            [
                packed(slot_ranks.reshape(-1), slot_rows.reshape(-1), slot_cols.reshape(-1)),
                packed(0, near_rows.reshape(-1), near_cols.reshape(-1)),
            ]
        ),
        near_blocks.reshape(near_blocks.shape[3:]),
        left_factors.reshape(left_factors.shape[3:]),
        right_factors.reshape(right_factors.shape[3:]),
    )
    share_shape = (group, order, leaf)
    message_shape = (group + 1, order, leaf)
    terms_shape = (col_count,) + share_shape

    (message,) = call(
        start_kernel, [message_shape], col_index.reshape(1), right_side, specs=[smem(), vmem()]
    )
    start_halves = gather_halves(message)
    start_factor, base, first_share, terms = apply_operator(
        start_mixes, 2, start_halves, start_halves, operator, terms_shape, jnp.float32
    )
    received = lax.all_to_all(terms, "cols", 0, 0)
    (share,) = call(sum_kernel, [share_shape], received)
    image_piece = spread_cols(share)
    (message,) = call(first_image_kernel, [message_shape], base, right_side, image_piece, share)
    image_halves = gather_halves(message)
    head, lower, top_inverse, own, mix, second_share, terms = apply_operator(
        middle_mixes,
        5,
        [*image_halves, base],
        image_halves + start_halves,
        operator,
        terms_shape,
        jnp.bfloat16,
    )
    received = lax.all_to_all(terms, "cols", 0, 0)
    (gram,) = call(
        second_image_kernel,
        [(order + order // 2, 2 * order)],
        first_share,
        second_share,
        received,
    )
    grams = spread_cols(reduce_rows_seg(gram))
    answer, hessen = call(
        final_kernel,
        [(order, cells), (3 * order, 2 * order)],
        grams,
        start_factor,
        head,
        lower,
        top_inverse,
        own,
        mix,
        base,
        right_side,
        image_piece,
    )
    return (answer, hessen)


def solution(mesh):
    in_specs = (
        P(None, ("rows", "seg")),
        P("rows", "seg", "cols", None, None, None),
        P("rows", "seg", "cols", None),
        P("rows", "seg", "cols", None),
        P("rows", "seg", "cols", None, None, None),
        P("rows", "seg", "cols", None, None, None),
        P("rows", "seg", "cols", None),
        P("rows", "seg", "cols", None),
        P("rows", "seg", "cols", None),
    )
    out_specs = (P(None, ("rows", "seg")), P())
    return jax.shard_map(body, mesh=mesh, in_specs=in_specs, out_specs=out_specs, check_vma=False)
```

time: 274 us -> 183 us (0.67)
  waiting for transfers between devices: 79.4 us -> 39.9 us
  Pallas kernels: 67.2 us -> 31.5 us
  blocking collectives: 40.8 us -> 74.5 us
  starting transfers between devices: 64.3 us -> 34.7 us
  local copies, waits for them, and re-layouts: 18.5 us -> 1.15 us
    all_to_all x3 -> x0, waiting for transfers between devices: 32.6 us -> none  [the longest x1 17.9 us: body(): received = lax.all_to_all(terms, 'cols', 0, 0)]
    pallas_call x7 -> x9, Pallas kernels: 28.3 us -> 8.34 us  [call(): pl.pallas_call(kernel, out_shape=tuple((jax.ShapeDtypeStruct(shape, jnp.f...]
    all_to_all x1 -> x2, blocking collectives: 20.4 us -> 39.4 us  [body(): received = lax.all_to_all(terms, 'cols', 0, 0)]
    pallas_call x2, Pallas kernels: 38.9 us -> 23.2 us  [apply_operator(): pl.pallas_call(functools.partial(apply_kernel, prepare, len(grams), small...]
    all_to_all x3 -> x0, starting transfers between devices: 15.8 us -> none  [the longest x1 8.21 us: body(): received = lax.all_to_all(terms, 'cols', 0, 0)]
    all_to_all x1 -> x2, blocking collectives: 20.4 us -> 35 us  [spread_cols(): lax.all_to_all(jnp.broadcast_to(values[None], (count,) + values.shape), '...]
    ppermute x35 -> x21, starting transfers between devices: 48.6 us -> 34.7 us  [exchange(): lax.ppermute(values, axis, [(at, at ^ distance) for at in range(count)])]
    unnamed x39 -> x16, local copies, waits for them, and re-layouts: 11.4 us -> 1.08 us
  transfers between devices with their start and end apart: 38 -> 21, of which waited for: 27 -> 14; matrix products, arithmetic and copies ran while one was open for 4% -> 0% of each run, Pallas kernels for 9% -> 0%
where the time goes in v2:
time: 183 us
  blocking collectives  74.5 us (41%)
  waiting for transfers between devices  39.9 us (22%)
  starting transfers between devices  34.7 us (19%)
  Pallas kernels  31.5 us (17%)
    ppermute x21, waiting for transfers between devices, exchange(): lax.ppermute(values, axis, [(at, at ^ distance) for at in range(count)])  39.9 us
    all_to_all x2, blocking collectives, body(): received = lax.all_to_all(terms, 'cols', 0, 0)  39.4 us
    all_to_all x2, blocking collectives, spread_cols(): lax.all_to_all(jnp.broadcast_to(values[None], (count,) + values.shape), '...  35 us
    ppermute x21, starting transfers between devices, exchange(): lax.ppermute(values, axis, [(at, at ^ distance) for at in range(count)])  34.7 us
    pallas_call x2, Pallas kernels, apply_operator(): pl.pallas_call(functools.partial(apply_kernel, prepare, len(grams), small...  23.2 us
    pallas_call x9, Pallas kernels, call(): pl.pallas_call(kernel, out_shape=tuple((jax.ShapeDtypeStruct(shape, jnp.f...  8.34 us
  transfers between devices with their start and end apart: 21, of which 14 were waited for; matrix products, arithmetic and copies ran while one was open for 0% of the time, Pallas kernels for 0%

profile of v2, /device:TPU:1, one launch (start us, length us, event | category | flops | bytes accessed | tf_op | source)
XLA Modules:
  0.0 182.6 jit_solution(14956761972206401064)
XLA Ops:
  0.6 0.0 copy-start
  0.6 1.0 copy-done
  1.7 0.6 shard_map.104.own_ref
  2.2 3.4 %collective-permute-start.2 = (f32[3,64,128]{2,1,0:T(8,128)S(1)}, f32[3,64,128]{2,1,0:T(8,128)S(1)}, u32[]{:S(2)}, u32[]{:S(2)}) collective-permute-start(f32[3,64,128]{2,1,0:T(8,128)S(1)} %shard_map.104.own_ref), channel_id=1, source_target_pairs={{0,3},{1,2},{2,1},{3,0},{4,7},{5,6},{6,5},{7,4},{8,11},{9,10},{10,... | collective-permute-start | bytes 294920 | tf_op jit(solution)/shard_map/ppermute | solution.py:374
  5.7 0.5 collective-permute-start.1
  6.2 0.2 collective-permute-start
  6.3 2.3 %collective-permute-done.2.three_ref = f32[3,64,128]{2,1,0:T(8,128)S(1)} collective-permute-done((f32[3,64,128]{2,1,0:T(8,128)S(1)}, f32[3,64,128]{2,1,0:T(8,128)S(1)}, u32[]{:S(2)}, u32[]{:S(2)}) %collective-permute-start.2) | collective-permute-done | bytes 98336 | tf_op jit(solution)/shard_map/ppermute | solution.py:374
  8.7 2.1 %collective-permute-done.1.two_ref = f32[3,64,128]{2,1,0:T(8,128)S(1)} collective-permute-done((f32[3,64,128]{2,1,0:T(8,128)S(1)}, f32[3,64,128]{2,1,0:T(8,128)S(1)}, u32[]{:S(2)}, u32[]{:S(2)}) %collective-permute-start.1) | collective-permute-done | bytes 98336 | tf_op jit(solution)/shard_map/ppermute | solution.py:374
  10.7 0.0 collective-permute-done.one_ref
  10.8 0.0 copy-start.6
  10.8 0.0 copy-start.7
  10.8 0.0 copy-start.3
  10.8 0.0 copy-start.4
  10.8 0.0 copy-start.5
  10.8 0.0 copy-start.2
  10.8 2.7 %collective-permute-start.5 = (f32[9,64,128]{2,1,0:T(8,128)S(1)}, f32[9,64,128]{2,1,0:T(8,128)S(1)}, u32[]{:S(2)}, u32[]{:S(2)}) collective-permute-start(f32[9,64,128]{2,1,0:T(8,128)S(1)} %shard_map.105.own_ref), channel_id=1, source_target_pairs={{0,192},{32,224},{64,128},{96,160},{128,64},{160,96},{192,0},{224,... | collective-permute-start | bytes 884744 | tf_op jit(solution)/shard_map/ppermute | solution.py:374
  13.6 0.3 collective-permute-start.4
  13.9 0.3 collective-permute-start.3
  14.2 11.9 %collective-permute-done.5.three_ref = f32[9,64,128]{2,1,0:T(8,128)S(1)} collective-permute-done((f32[9,64,128]{2,1,0:T(8,128)S(1)}, f32[9,64,128]{2,1,0:T(8,128)S(1)}, u32[]{:S(2)}, u32[]{:S(2)}) %collective-permute-start.5) | collective-permute-done | bytes 294944 | tf_op jit(solution)/shard_map/ppermute | solution.py:374
  26.1 0.0 collective-permute-done.4.two_ref
  26.1 0.0 collective-permute-done.3.one_ref
  26.1 0.1 shard_map.106.refs_0_.refs_2_.refs_5_
  26.2 2.5 %collective-permute-start.6 = (f32[33,64,128]{2,1,0:T(8,128)S(1)}, f32[33,64,128]{2,1,0:T(8,128)S(1)}, u32[]{:S(2)}, u32[]{:S(2)}) collective-permute-start(f32[33,64,128]{2,1,0:T(8,128)S(1)} %shard_map.106.refs_0_.refs_2_.refs_5_), channel_id=1, source_target_pairs={{0,32},{32,0},{64,96},{96,64},{128,160},{160,128},{192,224},{224,1... | collective-permute-start | bytes 3244040 | tf_op jit(solution)/shard_map/ppermute | solution.py:374
  28.7 0.0 copy-done.3
  28.8 0.0 copy-done.5
  28.8 2.2 %collective-permute-done.6.refs_1_.refs_3_.refs_6_ = f32[33,64,128]{2,1,0:T(8,128)S(1)} collective-permute-done((f32[33,64,128]{2,1,0:T(8,128)S(1)}, f32[33,64,128]{2,1,0:T(8,128)S(1)}, u32[]{:S(2)}, u32[]{:S(2)}) %collective-permute-start.6) | collective-permute-done | bytes 1081376 | tf_op jit(solution)/shard_map/ppermute | solution.py:374
  31.1 10.8 %shard_map.107 = (f32[64,64]{1,0:T(8,128)S(1)}, f32[64,64]{1,0:T(8,128)S(1)}, f32[2,64,128]{2,1,0:T(8,128)S(1)}, f32[8,2,64,128]{3,2,1,0:T(8,128)S(1)}) custom-call(s32[272]{0:T(512)S(1)} %pad_add_fusion.slots_ref, f32[33,64,128]{2,1,0:T(8,128)S(1)} %shard_map.106.refs_0_.refs_2_.refs_5_, f32[33,64,128]{2,1,0:T(8,128)S(1)} %collective-permute-done.6.refs_1_.refs_3_.refs_6_, ...), custom_call_target="tpu_custom_call" | custom-call | tf_op jit(solution)/shard_map/pallas_call | solution.py:338
  41.9 24.6 %all_to_all.20.terms_ref = f32[8,2,64,128]{3,2,1,0:T(8,128)S(1)} all-to-all(f32[8,2,64,128]{3,2,1,0:T(8,128)S(1)} %get-tuple-element.15), channel_id=1, replica_groups=mesh['rows'=8,'cols'=8,'seg'=4] {'cols'}, dimensions={0} | all-to-all | bytes 1048576 | tf_op jit(solution)/shard_map/all_to_all | solution.py:445
  66.6 17.2 %all_to_all.21.image_ref = f32[8,2,64,128]{3,2,1,0:T(8,128)S(1)} all-to-all(f32[8,2,64,128]{3,2,1,0:T(8,128)S(1)} %broadcast_in_dim.4), channel_id=1, replica_groups=mesh['rows'=8,'cols'=8,'seg'=4] {'cols'}, dimensions={0} | all-to-all | bytes 1048576 | tf_op jit(solution)/shard_map/all_to_all | solution.py:397
  83.8 1.5 shard_map.109.own_ref
  85.3 2.1 %collective-permute-start.9 = (f32[3,64,128]{2,1,0:T(8,128)S(1)}, f32[3,64,128]{2,1,0:T(8,128)S(1)}, u32[]{:S(2)}, u32[]{:S(2)}) collective-permute-start(f32[3,64,128]{2,1,0:T(8,128)S(1)} %shard_map.109.own_ref), channel_id=1, source_target_pairs={{0,3},{1,2},{2,1},{3,0},{4,7},{5,6},{6,5},{7,4},{8,11},{9,10},{10,... | collective-permute-start | bytes 294920 | tf_op jit(solution)/shard_map/ppermute | solution.py:374
  87.5 0.7 collective-permute-start.8
  88.2 0.5 collective-permute-start.7
  88.7 1.4 collective-permute-done.9.three_ref
  90.1 2.4 %collective-permute-done.8.two_ref = f32[3,64,128]{2,1,0:T(8,128)S(1)} collective-permute-done((f32[3,64,128]{2,1,0:T(8,128)S(1)}, f32[3,64,128]{2,1,0:T(8,128)S(1)}, u32[]{:S(2)}, u32[]{:S(2)}) %collective-permute-start.8) | collective-permute-done | bytes 98336 | tf_op jit(solution)/shard_map/ppermute | solution.py:374
  92.5 0.0 collective-permute-done.7.one_ref
  92.5 2.7 %collective-permute-start.12 = (f32[9,64,128]{2,1,0:T(8,128)S(1)}, f32[9,64,128]{2,1,0:T(8,128)S(1)}, u32[]{:S(2)}, u32[]{:S(2)}) collective-permute-start(f32[9,64,128]{2,1,0:T(8,128)S(1)} %shard_map.110.own_ref), channel_id=1, source_target_pairs={{0,192},{32,224},{64,128},{96,160},{128,64},{160,96},{192,0},{224,... | collective-permute-start | bytes 884744 | tf_op jit(solution)/shard_map/ppermute | solution.py:374
  95.2 0.8 collective-permute-start.11
  96.0 0.0 collective-permute-start.10
  96.0 6.8 %collective-permute-done.12.three_ref = f32[9,64,128]{2,1,0:T(8,128)S(1)} collective-permute-done((f32[9,64,128]{2,1,0:T(8,128)S(1)}, f32[9,64,128]{2,1,0:T(8,128)S(1)}, u32[]{:S(2)}, u32[]{:S(2)}) %collective-permute-start.12) | collective-permute-done | bytes 294944 | tf_op jit(solution)/shard_map/ppermute | solution.py:374
  102.9 0.0 collective-permute-done.11.two_ref
  102.9 1.0 collective-permute-done.10.one_ref
  103.8 0.1 shard_map.111.refs_0_.refs_3_
  103.9 6.5 %collective-permute-start.13 = (f32[33,64,128]{2,1,0:T(8,128)S(1)}, f32[33,64,128]{2,1,0:T(8,128)S(1)}, u32[]{:S(2)}, u32[]{:S(2)}) collective-permute-start(f32[33,64,128]{2,1,0:T(8,128)S(1)} %shard_map.111.refs_0_.refs_3_), channel_id=1, source_target_pairs={{0,32},{32,0},{64,96},{96,64},{128,160},{160,128},{192,224},{224,1... | collective-permute-start | bytes 3244040 | tf_op jit(solution)/shard_map/ppermute | solution.py:374
  110.5 2.3 %collective-permute-done.13.refs_1_.refs_4_ = f32[33,64,128]{2,1,0:T(8,128)S(1)} collective-permute-done((f32[33,64,128]{2,1,0:T(8,128)S(1)}, f32[33,64,128]{2,1,0:T(8,128)S(1)}, u32[]{:S(2)}, u32[]{:S(2)}) %collective-permute-start.13) | collective-permute-done | bytes 1081376 | tf_op jit(solution)/shard_map/ppermute | solution.py:374
  112.8 12.4 %shard_map.112 = (f32[64,64]{1,0:T(8,128)S(1)}, f32[64,64]{1,0:T(8,128)S(1)}, f32[64,64]{1,0:T(8,128)S(1)}, f32[64,64]{1,0:T(8,128)S(1)}, f32[64,64]{1,0:T(8,128...) custom-call(s32[272]{0:T(512)S(1)} %pad_add_fusion.slots_ref, ...), custom_call_target="tpu_custom_call" | custom-call | tf_op jit(solution)/shard_map/pallas_call | solution.py:338
  125.1 14.8 %all_to_all.22.terms_ref = bf16[8,2,64,128]{3,2,1,0:T(8,128)(2,1)S(1)} all-to-all(bf16[8,2,64,128]{3,2,1,0:T(8,128)(2,1)S(1)} %get-tuple-element.17), channel_id=1, replica_groups=mesh['rows'=8,'cols'=8,'seg'=4] {'cols'}, dimensions={0} | all-to-all | bytes 524288 | tf_op jit(solution)/shard_map/all_to_all | solution.py:459
  140.0 0.5 shard_map.113
  140.5 1.6 collective-permute-start.16
  142.1 0.5 collective-permute-start.15
  142.7 1.2 collective-permute-start.14
  143.8 0.9 collective-permute-done.16
  144.7 1.9 %collective-permute-done.15 = f32[96,128]{1,0:T(8,128)S(1)} collective-permute-done((f32[96,128]{1,0:T(8,128)S(1)}, f32[96,128]{1,0:T(8,128)S(1)}, u32[]{:S(2)}, u32[]{:S(2)}) %collective-permute-start.15) | collective-permute-done | bytes 49184 | tf_op jit(solution)/shard_map/ppermute | solution.py:374
  146.6 0.0 collective-permute-done.14
  146.6 2.7 %collective-permute-start.19 = (f32[96,128]{1,0:T(8,128)S(1)}, f32[96,128]{1,0:T(8,128)S(1)}, u32[]{:S(2)}, u32[]{:S(2)}) collective-permute-start(f32[96,128]{1,0:T(8,128)S(1)} %add_add_fusion.1), channel_id=1, source_target_pairs={{0,192},{32,224},{64,128},{96,160},{128,64},{160,96},{192,0},{224,... | collective-permute-start | bytes 147464 | tf_op jit(solution)/shard_map/ppermute | solution.py:374
  149.3 0.5 collective-permute-start.18
  149.8 0.2 collective-permute-start.17
  150.0 0.9 collective-permute-done.19
  150.9 2.9 %collective-permute-done.18 = f32[96,128]{1,0:T(8,128)S(1)} collective-permute-done((f32[96,128]{1,0:T(8,128)S(1)}, f32[96,128]{1,0:T(8,128)S(1)}, u32[]{:S(2)}, u32[]{:S(2)}) %collective-permute-start.18) | collective-permute-done | bytes 49184 | tf_op jit(solution)/shard_map/ppermute | solution.py:374
  153.8 0.0 collective-permute-done.17
  153.8 4.6 %collective-permute-start.20 = (f32[96,128]{1,0:T(8,128)S(1)}, f32[96,128]{1,0:T(8,128)S(1)}, u32[]{:S(2)}, u32[]{:S(2)}) collective-permute-start(f32[96,128]{1,0:T(8,128)S(1)} %add_add_fusion), channel_id=1, source_target_pairs={{0,32},{32,0},{64,96},{96,64},{128,160},{160,128},{192,224},{224,1... | collective-permute-start | bytes 147464 | tf_op jit(solution)/shard_map/ppermute | solution.py:374
  158.4 0.9 collective-permute-done.20
  159.3 17.8 %all_to_all.23.grams_ref = f32[8,96,128]{2,1,0:T(8,128)S(1)} all-to-all(f32[8,96,128]{2,1,0:T(8,128)S(1)} %broadcast_in_dim.5), channel_id=1, replica_groups=mesh['rows'=8,'cols'=8,'seg'=4] {'cols'}, dimensions={0} | all-to-all | bytes 786432 | tf_op jit(solution)/shard_map/all_to_all | solution.py:397
  177.1 5.5 %shard_map.114 = (f32[64,2048]{1,0:T(8,128)}, f32[192,128]{1,0:T(8,128)}) custom-call(f32[8,96,128]{2,1,0:T(8,128)S(1)} %all_to_all.23.grams_ref, f32[64,64]{1,0:T(8,128)S(1)} %get-tuple-element.18.start_ref, f32[64,64]{1,0:T(8,128)S(1)} %get-tuple-element.19.head_ref, f32[64,64]{1,0:T(8,128)S(1)} %get-tuple-element.20.lower_ref, ...), custom_call_target="tpu_custom_call" | custom-call | tf_op jit(solution)/shard_map/pallas_call | solution.py:363
  (18 shorter events, 0.3 us)
Async XLA Ops:
  0.6 1.0 copy-start
  2.2 6.4 %collective-permute-start.2 = (f32[3,64,128]{2,1,0:T(8,128)S(1)}, f32[3,64,128]{2,1,0:T(8,128)S(1)}, u32[]{:S(2)}, u32[]{:S(2)}) collective-permute-start(f32[3,64,128]{2,1,0:T(8,128)S(1)} %shard_map.104.own_ref), channel_id=1, source_target_pairs={{0,3},{1,2},{2,1},{3,0},{4,7},{5,6},{6,5},{7,4},{8,11},{9,10},{10,... | collective-permute-start | bytes 294920 | tf_op jit(solution)/shard_map/ppermute | solution.py:374
  5.7 5.1 %collective-permute-start.1 = (f32[3,64,128]{2,1,0:T(8,128)S(1)}, f32[3,64,128]{2,1,0:T(8,128)S(1)}, u32[]{:S(2)}, u32[]{:S(2)}) collective-permute-start(f32[3,64,128]{2,1,0:T(8,128)S(1)} %shard_map.104.own_ref), channel_id=1, source_target_pairs={{0,2},{1,3},{2,0},{3,1},{4,6},{5,7},{6,4},{7,5},{8,10},{9,11},{10,... | collective-permute-start | bytes 294920 | tf_op jit(solution)/shard_map/ppermute | solution.py:374
  6.2 4.6 %collective-permute-start = (f32[3,64,128]{2,1,0:T(8,128)S(1)}, f32[3,64,128]{2,1,0:T(8,128)S(1)}, u32[]{:S(2)}, u32[]{:S(2)}) collective-permute-start(f32[3,64,128]{2,1,0:T(8,128)S(1)} %shard_map.104.own_ref), channel_id=1, source_target_pairs={{0,1},{1,0},{2,3},{3,2},{4,5},{5,4},{6,7},{7,6},{8,9},{9,8},{10,11... | collective-permute-start | bytes 294920 | tf_op jit(solution)/shard_map/ppermute | solution.py:374
  10.8 18.0 %copy-start.6 = (s32[1,1,1,16]{3,2,1,0:T(1,128)S(1)}, s32[1,1,1,16]{3,2,1,0:T(1,128)}, u32[]{:S(2)}) copy-start(s32[1,1,1,16]{3,2,1,0:T(1,128)} %param.12) | copy-start | bytes 196
  10.8 18.0 %copy-start.7 = (s32[1,1,1,16]{3,2,1,0:T(1,128)S(1)}, s32[1,1,1,16]{3,2,1,0:T(1,128)}, u32[]{:S(2)}) copy-start(s32[1,1,1,16]{3,2,1,0:T(1,128)} %param.11) | copy-start | bytes 196
  10.8 18.0 %copy-start.3 = (s32[1,1,1,256]{3,2,1,0:T(1,128)S(1)}, s32[1,1,1,256]{3,2,1,0:T(1,128)}, u32[]{:S(2)}) copy-start(s32[1,1,1,256]{3,2,1,0:T(1,128)} %param.16) | copy-start | bytes 3076
  10.8 18.0 %copy-start.4 = (s32[1,1,1,256]{3,2,1,0:T(1,128)S(1)}, s32[1,1,1,256]{3,2,1,0:T(1,128)}, u32[]{:S(2)}) copy-start(s32[1,1,1,256]{3,2,1,0:T(1,128)} %param.15) | copy-start | bytes 3076
  10.8 18.0 %copy-start.5 = (s32[1,1,1,256]{3,2,1,0:T(1,128)S(1)}, s32[1,1,1,256]{3,2,1,0:T(1,128)}, u32[]{:S(2)}) copy-start(s32[1,1,1,256]{3,2,1,0:T(1,128)} %param.17) | copy-start | bytes 3076
  10.8 20.2 %copy-start.2 = (bf16[1,1,1,16,128,128]{5,4,3,2,1,0:T(8,128)(2,1)S(1)}, bf16[1,1,1,16,128,128]{5,4,3,2,1,0:T(8,128)(2,1)}, u32[]{:S(2)}) copy-start(bf16[1,1,1,16,128,128]{5,4,3,2,1,0:T(8,128)(2,1)} %param.10) | copy-start | bytes 1572868
  10.8 15.3 %collective-permute-start.5 = (f32[9,64,128]{2,1,0:T(8,128)S(1)}, f32[9,64,128]{2,1,0:T(8,128)S(1)}, u32[]{:S(2)}, u32[]{:S(2)}) collective-permute-start(f32[9,64,128]{2,1,0:T(8,128)S(1)} %shard_map.105.own_ref), channel_id=1, source_target_pairs={{0,192},{32,224},{64,128},{96,160},{128,64},{160,96},{192,0},{224,... | collective-permute-start | bytes 884744 | tf_op jit(solution)/shard_map/ppermute | solution.py:374
  13.6 12.6 %collective-permute-start.4 = (f32[9,64,128]{2,1,0:T(8,128)S(1)}, f32[9,64,128]{2,1,0:T(8,128)S(1)}, u32[]{:S(2)}, u32[]{:S(2)}) collective-permute-start(f32[9,64,128]{2,1,0:T(8,128)S(1)} %shard_map.105.own_ref), channel_id=1, source_target_pairs={{0,128},{32,160},{64,192},{96,224},{128,0},{160,32},{192,64},{224,... | collective-permute-start | bytes 884744 | tf_op jit(solution)/shard_map/ppermute | solution.py:374
  13.9 12.2 %collective-permute-start.3 = (f32[9,64,128]{2,1,0:T(8,128)S(1)}, f32[9,64,128]{2,1,0:T(8,128)S(1)}, u32[]{:S(2)}, u32[]{:S(2)}) collective-permute-start(f32[9,64,128]{2,1,0:T(8,128)S(1)} %shard_map.105.own_ref), channel_id=1, source_target_pairs={{0,64},{32,96},{64,0},{96,32},{128,192},{160,224},{192,128},{224,1... | collective-permute-start | bytes 884744 | tf_op jit(solution)/shard_map/ppermute | solution.py:374
  26.2 4.8 %collective-permute-start.6 = (f32[33,64,128]{2,1,0:T(8,128)S(1)}, f32[33,64,128]{2,1,0:T(8,128)S(1)}, u32[]{:S(2)}, u32[]{:S(2)}) collective-permute-start(f32[33,64,128]{2,1,0:T(8,128)S(1)} %shard_map.106.refs_0_.refs_2_.refs_5_), channel_id=1, source_target_pairs={{0,32},{32,0},{64,96},{96,64},{128,160},{160,128},{192,224},{224,1... | collective-permute-start | bytes 3244040 | tf_op jit(solution)/shard_map/ppermute | solution.py:374
  66.5 17.3 %copy-start.1 = (f32[64,2048]{1,0:T(8,128)S(1)}, f32[64,2048]{1,0:T(8,128)}, u32[]{:S(2)}) copy-start(f32[64,2048]{1,0:T(8,128)} %right_ref.3) | copy-start | bytes 1572868
  85.3 4.8 %collective-permute-start.9 = (f32[3,64,128]{2,1,0:T(8,128)S(1)}, f32[3,64,128]{2,1,0:T(8,128)S(1)}, u32[]{:S(2)}, u32[]{:S(2)}) collective-permute-start(f32[3,64,128]{2,1,0:T(8,128)S(1)} %shard_map.109.own_ref), channel_id=1, source_target_pairs={{0,3},{1,2},{2,1},{3,0},{4,7},{5,6},{6,5},{7,4},{8,11},{9,10},{10,... | collective-permute-start | bytes 294920 | tf_op jit(solution)/shard_map/ppermute | solution.py:374
  87.5 5.0 %collective-permute-start.8 = (f32[3,64,128]{2,1,0:T(8,128)S(1)}, f32[3,64,128]{2,1,0:T(8,128)S(1)}, u32[]{:S(2)}, u32[]{:S(2)}) collective-permute-start(f32[3,64,128]{2,1,0:T(8,128)S(1)} %shard_map.109.own_ref), channel_id=1, source_target_pairs={{0,2},{1,3},{2,0},{3,1},{4,6},{5,7},{6,4},{7,5},{8,10},{9,11},{10,... | collective-permute-start | bytes 294920 | tf_op jit(solution)/shard_map/ppermute | solution.py:374
  88.2 4.2 %collective-permute-start.7 = (f32[3,64,128]{2,1,0:T(8,128)S(1)}, f32[3,64,128]{2,1,0:T(8,128)S(1)}, u32[]{:S(2)}, u32[]{:S(2)}) collective-permute-start(f32[3,64,128]{2,1,0:T(8,128)S(1)} %shard_map.109.own_ref), channel_id=1, source_target_pairs={{0,1},{1,0},{2,3},{3,2},{4,5},{5,4},{6,7},{7,6},{8,9},{9,8},{10,11... | collective-permute-start | bytes 294920 | tf_op jit(solution)/shard_map/ppermute | solution.py:374
  92.5 10.4 %collective-permute-start.12 = (f32[9,64,128]{2,1,0:T(8,128)S(1)}, f32[9,64,128]{2,1,0:T(8,128)S(1)}, u32[]{:S(2)}, u32[]{:S(2)}) collective-permute-start(f32[9,64,128]{2,1,0:T(8,128)S(1)} %shard_map.110.own_ref), channel_id=1, source_target_pairs={{0,192},{32,224},{64,128},{96,160},{128,64},{160,96},{192,0},{224,... | collective-permute-start | bytes 884744 | tf_op jit(solution)/shard_map/ppermute | solution.py:374
  95.2 7.6 %collective-permute-start.11 = (f32[9,64,128]{2,1,0:T(8,128)S(1)}, f32[9,64,128]{2,1,0:T(8,128)S(1)}, u32[]{:S(2)}, u32[]{:S(2)}) collective-permute-start(f32[9,64,128]{2,1,0:T(8,128)S(1)} %shard_map.110.own_ref), channel_id=1, source_target_pairs={{0,128},{32,160},{64,192},{96,224},{128,0},{160,32},{192,64},{224,... | collective-permute-start | bytes 884744 | tf_op jit(solution)/shard_map/ppermute | solution.py:374
  96.0 7.8 %collective-permute-start.10 = (f32[9,64,128]{2,1,0:T(8,128)S(1)}, f32[9,64,128]{2,1,0:T(8,128)S(1)}, u32[]{:S(2)}, u32[]{:S(2)}) collective-permute-start(f32[9,64,128]{2,1,0:T(8,128)S(1)} %shard_map.110.own_ref), channel_id=1, source_target_pairs={{0,64},{32,96},{64,0},{96,32},{128,192},{160,224},{192,128},{224,1... | collective-permute-start | bytes 884744 | tf_op jit(solution)/shard_map/ppermute | solution.py:374
  103.9 8.9 %collective-permute-start.13 = (f32[33,64,128]{2,1,0:T(8,128)S(1)}, f32[33,64,128]{2,1,0:T(8,128)S(1)}, u32[]{:S(2)}, u32[]{:S(2)}) collective-permute-start(f32[33,64,128]{2,1,0:T(8,128)S(1)} %shard_map.111.refs_0_.refs_3_), channel_id=1, source_target_pairs={{0,32},{32,0},{64,96},{96,64},{128,160},{160,128},{192,224},{224,1... | collective-permute-start | bytes 3244040 | tf_op jit(solution)/shard_map/ppermute | solution.py:374
  140.5 4.2 %collective-permute-start.16 = (f32[96,128]{1,0:T(8,128)S(1)}, f32[96,128]{1,0:T(8,128)S(1)}, u32[]{:S(2)}, u32[]{:S(2)}) collective-permute-start(f32[96,128]{1,0:T(8,128)S(1)} %shard_map.113), channel_id=1, source_target_pairs={{0,3},{1,2},{2,1},{3,0},{4,7},{5,6},{6,5},{7,4},{8,11},{9,10},{10,... | collective-permute-start | bytes 147464 | tf_op jit(solution)/shard_map/ppermute | solution.py:374
  142.1 4.5 %collective-permute-start.15 = (f32[96,128]{1,0:T(8,128)S(1)}, f32[96,128]{1,0:T(8,128)S(1)}, u32[]{:S(2)}, u32[]{:S(2)}) collective-permute-start(f32[96,128]{1,0:T(8,128)S(1)} %shard_map.113), channel_id=1, source_target_pairs={{0,2},{1,3},{2,0},{3,1},{4,6},{5,7},{6,4},{7,5},{8,10},{9,11},{10,... | collective-permute-start | bytes 147464 | tf_op jit(solution)/shard_map/ppermute | solution.py:374
  142.7 3.9 %collective-permute-start.14 = (f32[96,128]{1,0:T(8,128)S(1)}, f32[96,128]{1,0:T(8,128)S(1)}, u32[]{:S(2)}, u32[]{:S(2)}) collective-permute-start(f32[96,128]{1,0:T(8,128)S(1)} %shard_map.113), channel_id=1, source_target_pairs={{0,1},{1,0},{2,3},{3,2},{4,5},{5,4},{6,7},{7,6},{8,9},{9,8},{10,11... | collective-permute-start | bytes 147464 | tf_op jit(solution)/shard_map/ppermute | solution.py:374
  146.6 4.2 %collective-permute-start.19 = (f32[96,128]{1,0:T(8,128)S(1)}, f32[96,128]{1,0:T(8,128)S(1)}, u32[]{:S(2)}, u32[]{:S(2)}) collective-permute-start(f32[96,128]{1,0:T(8,128)S(1)} %add_add_fusion.1), channel_id=1, source_target_pairs={{0,192},{32,224},{64,128},{96,160},{128,64},{160,96},{192,0},{224,... | collective-permute-start | bytes 147464 | tf_op jit(solution)/shard_map/ppermute | solution.py:374
  149.3 4.4 %collective-permute-start.18 = (f32[96,128]{1,0:T(8,128)S(1)}, f32[96,128]{1,0:T(8,128)S(1)}, u32[]{:S(2)}, u32[]{:S(2)}) collective-permute-start(f32[96,128]{1,0:T(8,128)S(1)} %add_add_fusion.1), channel_id=1, source_target_pairs={{0,128},{32,160},{64,192},{96,224},{128,0},{160,32},{192,64},{224,... | collective-permute-start | bytes 147464 | tf_op jit(solution)/shard_map/ppermute | solution.py:374
  149.8 3.9 %collective-permute-start.17 = (f32[96,128]{1,0:T(8,128)S(1)}, f32[96,128]{1,0:T(8,128)S(1)}, u32[]{:S(2)}, u32[]{:S(2)}) collective-permute-start(f32[96,128]{1,0:T(8,128)S(1)} %add_add_fusion.1), channel_id=1, source_target_pairs={{0,64},{32,96},{64,0},{96,32},{128,192},{160,224},{192,128},{224,1... | collective-permute-start | bytes 147464 | tf_op jit(solution)/shard_map/ppermute | solution.py:374
  153.8 5.5 %collective-permute-start.20 = (f32[96,128]{1,0:T(8,128)S(1)}, f32[96,128]{1,0:T(8,128)S(1)}, u32[]{:S(2)}, u32[]{:S(2)}) collective-permute-start(f32[96,128]{1,0:T(8,128)S(1)} %add_add_fusion), channel_id=1, source_target_pairs={{0,32},{32,0},{64,96},{96,64},{128,160},{160,128},{192,224},{224,1... | collective-permute-start | bytes 147464 | tf_op jit(solution)/shard_map/ppermute | solution.py:374

commit v3 on v2

--- a/solution.py
+++ b/solution.py
@@ -11,8 +11,8 @@
 NN = (((1,), (0,)), ((), ()))
 NT = (((1,), (1,)), ((), ()))
 TN = (((0,), (0,)), ((), ()))
-CHUNKS = 8
-UNROLL = 32
+CHUNKS = 4
+UNROLL = 64
 VMEM_LIMIT = 48 * 1024 * 1024
 
 

time: 183 us -> 181 us (0.989)
  no operation moved by 1% of the time
where the time goes in v3:
time: 181 us
  blocking collectives  73.6 us (41%)
  waiting for transfers between devices  40.5 us (22%)
  starting transfers between devices  34.5 us (19%)
  Pallas kernels  30.5 us (17%)
    ppermute x21, waiting for transfers between devices, exchange(): lax.ppermute(values, axis, [(at, at ^ distance) for at in range(count)])  40.5 us
    all_to_all x2, blocking collectives, body(): received = lax.all_to_all(terms, 'cols', 0, 0)  39.2 us
    all_to_all x2, blocking collectives, spread_cols(): lax.all_to_all(jnp.broadcast_to(values[None], (count,) + values.shape), '...  34.5 us
    ppermute x21, starting transfers between devices, exchange(): lax.ppermute(values, axis, [(at, at ^ distance) for at in range(count)])  34.5 us
    pallas_call x2, Pallas kernels, apply_operator(): pl.pallas_call(functools.partial(apply_kernel, prepare, len(grams), small...  22.2 us
    pallas_call x9, Pallas kernels, call(): pl.pallas_call(kernel, out_shape=tuple((jax.ShapeDtypeStruct(shape, jnp.f...  8.34 us
  transfers between devices with their start and end apart: 21, of which 14 were waited for; matrix products, arithmetic and copies ran while one was open for 0% of the time, Pallas kernels for 0%

profile of v3, /device:TPU:1, one launch (start us, length us, event | category | flops | bytes accessed | tf_op | source)
XLA Modules:
  0.0 181.2 jit_solution(9769888236049691070)
XLA Ops:
  0.6 0.0 copy-start
  0.6 1.0 copy-done
  1.7 0.6 shard_map.104.own_ref
  2.2 3.4 %collective-permute-start.2 = (f32[3,64,128]{2,1,0:T(8,128)S(1)}, f32[3,64,128]{2,1,0:T(8,128)S(1)}, u32[]{:S(2)}, u32[]{:S(2)}) collective-permute-start(f32[3,64,128]{2,1,0:T(8,128)S(1)} %shard_map.104.own_ref), channel_id=1, source_target_pairs={{0,3},{1,2},{2,1},{3,0},{4,7},{5,6},{6,5},{7,4},{8,11},{9,10},{10,... | collective-permute-start | bytes 294920 | tf_op jit(solution)/shard_map/ppermute | solution.py:374
  5.7 0.5 collective-permute-start.1
  6.2 0.2 collective-permute-start
  6.3 2.3 %collective-permute-done.2.three_ref = f32[3,64,128]{2,1,0:T(8,128)S(1)} collective-permute-done((f32[3,64,128]{2,1,0:T(8,128)S(1)}, f32[3,64,128]{2,1,0:T(8,128)S(1)}, u32[]{:S(2)}, u32[]{:S(2)}) %collective-permute-start.2) | collective-permute-done | bytes 98336 | tf_op jit(solution)/shard_map/ppermute | solution.py:374
  8.7 2.1 %collective-permute-done.1.two_ref = f32[3,64,128]{2,1,0:T(8,128)S(1)} collective-permute-done((f32[3,64,128]{2,1,0:T(8,128)S(1)}, f32[3,64,128]{2,1,0:T(8,128)S(1)}, u32[]{:S(2)}, u32[]{:S(2)}) %collective-permute-start.1) | collective-permute-done | bytes 98336 | tf_op jit(solution)/shard_map/ppermute | solution.py:374
  10.7 0.0 collective-permute-done.one_ref
  10.8 0.0 copy-start.6
  10.8 0.0 copy-start.7
  10.8 0.0 copy-start.3
  10.8 0.0 copy-start.4
  10.8 0.0 copy-start.5
  10.8 0.0 copy-start.2
  10.8 2.7 %collective-permute-start.5 = (f32[9,64,128]{2,1,0:T(8,128)S(1)}, f32[9,64,128]{2,1,0:T(8,128)S(1)}, u32[]{:S(2)}, u32[]{:S(2)}) collective-permute-start(f32[9,64,128]{2,1,0:T(8,128)S(1)} %shard_map.105.own_ref), channel_id=1, source_target_pairs={{0,192},{32,224},{64,128},{96,160},{128,64},{160,96},{192,0},{224,... | collective-permute-start | bytes 884744 | tf_op jit(solution)/shard_map/ppermute | solution.py:374
  13.6 0.3 collective-permute-start.4
  13.9 0.3 collective-permute-start.3
  14.2 11.9 %collective-permute-done.5.three_ref = f32[9,64,128]{2,1,0:T(8,128)S(1)} collective-permute-done((f32[9,64,128]{2,1,0:T(8,128)S(1)}, f32[9,64,128]{2,1,0:T(8,128)S(1)}, u32[]{:S(2)}, u32[]{:S(2)}) %collective-permute-start.5) | collective-permute-done | bytes 294944 | tf_op jit(solution)/shard_map/ppermute | solution.py:374
  26.1 0.0 collective-permute-done.4.two_ref
  26.1 0.0 collective-permute-done.3.one_ref
  26.1 0.1 shard_map.106.refs_0_.refs_2_.refs_5_
  26.2 2.5 %collective-permute-start.6 = (f32[33,64,128]{2,1,0:T(8,128)S(1)}, f32[33,64,128]{2,1,0:T(8,128)S(1)}, u32[]{:S(2)}, u32[]{:S(2)}) collective-permute-start(f32[33,64,128]{2,1,0:T(8,128)S(1)} %shard_map.106.refs_0_.refs_2_.refs_5_), channel_id=1, source_target_pairs={{0,32},{32,0},{64,96},{96,64},{128,160},{160,128},{192,224},{224,1... | collective-permute-start | bytes 3244040 | tf_op jit(solution)/shard_map/ppermute | solution.py:374
  28.7 0.0 copy-done.7
  28.8 0.0 copy-done.4
  28.8 2.2 %collective-permute-done.6.refs_1_.refs_3_.refs_6_ = f32[33,64,128]{2,1,0:T(8,128)S(1)} collective-permute-done((f32[33,64,128]{2,1,0:T(8,128)S(1)}, f32[33,64,128]{2,1,0:T(8,128)S(1)}, u32[]{:S(2)}, u32[]{:S(2)}) %collective-permute-start.6) | collective-permute-done | bytes 1081376 | tf_op jit(solution)/shard_map/ppermute | solution.py:374
  31.1 10.3 %shard_map.107 = (f32[64,64]{1,0:T(8,128)S(1)}, f32[64,64]{1,0:T(8,128)S(1)}, f32[2,64,128]{2,1,0:T(8,128)S(1)}, f32[8,2,64,128]{3,2,1,0:T(8,128)S(1)}) custom-call(s32[272]{0:T(512)S(1)} %pad_add_fusion.slots_ref, f32[33,64,128]{2,1,0:T(8,128)S(1)} %shard_map.106.refs_0_.refs_2_.refs_5_, f32[33,64,128]{2,1,0:T(8,128)S(1)} %collective-permute-done.6.refs_1_.refs_3_.refs_6_, ...), custom_call_target="tpu_custom_call" | custom-call | tf_op jit(solution)/shard_map/pallas_call | solution.py:338
  41.4 24.5 %all_to_all.20.terms_ref = f32[8,2,64,128]{3,2,1,0:T(8,128)S(1)} all-to-all(f32[8,2,64,128]{3,2,1,0:T(8,128)S(1)} %get-tuple-element.15), channel_id=1, replica_groups=mesh['rows'=8,'cols'=8,'seg'=4] {'cols'}, dimensions={0} | all-to-all | bytes 1048576 | tf_op jit(solution)/shard_map/all_to_all | solution.py:445
  66.0 17.1 %all_to_all.21.image_ref = f32[8,2,64,128]{3,2,1,0:T(8,128)S(1)} all-to-all(f32[8,2,64,128]{3,2,1,0:T(8,128)S(1)} %broadcast_in_dim.4), channel_id=1, replica_groups=mesh['rows'=8,'cols'=8,'seg'=4] {'cols'}, dimensions={0} | all-to-all | bytes 1048576 | tf_op jit(solution)/shard_map/all_to_all | solution.py:397
  83.1 1.5 shard_map.109.own_ref
  84.6 2.8 %collective-permute-start.9 = (f32[3,64,128]{2,1,0:T(8,128)S(1)}, f32[3,64,128]{2,1,0:T(8,128)S(1)}, u32[]{:S(2)}, u32[]{:S(2)}) collective-permute-start(f32[3,64,128]{2,1,0:T(8,128)S(1)} %shard_map.109.own_ref), channel_id=1, source_target_pairs={{0,3},{1,2},{2,1},{3,0},{4,7},{5,6},{6,5},{7,4},{8,11},{9,10},{10,... | collective-permute-start | bytes 294920 | tf_op jit(solution)/shard_map/ppermute | solution.py:374
  87.4 0.3 collective-permute-start.8
  87.7 0.4 collective-permute-start.7
  88.0 1.9 %collective-permute-done.9.three_ref = f32[3,64,128]{2,1,0:T(8,128)S(1)} collective-permute-done((f32[3,64,128]{2,1,0:T(8,128)S(1)}, f32[3,64,128]{2,1,0:T(8,128)S(1)}, u32[]{:S(2)}, u32[]{:S(2)}) %collective-permute-start.9) | collective-permute-done | bytes 98336 | tf_op jit(solution)/shard_map/ppermute | solution.py:374
  90.0 2.4 %collective-permute-done.8.two_ref = f32[3,64,128]{2,1,0:T(8,128)S(1)} collective-permute-done((f32[3,64,128]{2,1,0:T(8,128)S(1)}, f32[3,64,128]{2,1,0:T(8,128)S(1)}, u32[]{:S(2)}, u32[]{:S(2)}) %collective-permute-start.8) | collective-permute-done | bytes 98336 | tf_op jit(solution)/shard_map/ppermute | solution.py:374
  92.3 0.0 collective-permute-done.7.one_ref
  92.4 2.3 %collective-permute-start.12 = (f32[9,64,128]{2,1,0:T(8,128)S(1)}, f32[9,64,128]{2,1,0:T(8,128)S(1)}, u32[]{:S(2)}, u32[]{:S(2)}) collective-permute-start(f32[9,64,128]{2,1,0:T(8,128)S(1)} %shard_map.110.own_ref), channel_id=1, source_target_pairs={{0,192},{32,224},{64,128},{96,160},{128,64},{160,96},{192,0},{224,... | collective-permute-start | bytes 884744 | tf_op jit(solution)/shard_map/ppermute | solution.py:374
  94.7 0.9 collective-permute-start.11
  95.6 0.1 collective-permute-start.10
  95.7 7.5 %collective-permute-done.12.three_ref = f32[9,64,128]{2,1,0:T(8,128)S(1)} collective-permute-done((f32[9,64,128]{2,1,0:T(8,128)S(1)}, f32[9,64,128]{2,1,0:T(8,128)S(1)}, u32[]{:S(2)}, u32[]{:S(2)}) %collective-permute-start.12) | collective-permute-done | bytes 294944 | tf_op jit(solution)/shard_map/ppermute | solution.py:374
  103.2 0.0 collective-permute-done.11.two_ref
  103.2 0.6 collective-permute-done.10.one_ref
  103.8 0.1 shard_map.111.refs_0_.refs_3_
  103.9 6.3 %collective-permute-start.13 = (f32[33,64,128]{2,1,0:T(8,128)S(1)}, f32[33,64,128]{2,1,0:T(8,128)S(1)}, u32[]{:S(2)}, u32[]{:S(2)}) collective-permute-start(f32[33,64,128]{2,1,0:T(8,128)S(1)} %shard_map.111.refs_0_.refs_3_), channel_id=1, source_target_pairs={{0,32},{32,0},{64,96},{96,64},{128,160},{160,128},{192,224},{224,1... | collective-permute-start | bytes 3244040 | tf_op jit(solution)/shard_map/ppermute | solution.py:374
  110.3 2.3 %collective-permute-done.13.refs_1_.refs_4_ = f32[33,64,128]{2,1,0:T(8,128)S(1)} collective-permute-done((f32[33,64,128]{2,1,0:T(8,128)S(1)}, f32[33,64,128]{2,1,0:T(8,128)S(1)}, u32[]{:S(2)}, u32[]{:S(2)}) %collective-permute-start.13) | collective-permute-done | bytes 1081376 | tf_op jit(solution)/shard_map/ppermute | solution.py:374
  112.6 11.9 %shard_map.112 = (f32[64,64]{1,0:T(8,128)S(1)}, f32[64,64]{1,0:T(8,128)S(1)}, f32[64,64]{1,0:T(8,128)S(1)}, f32[64,64]{1,0:T(8,128)S(1)}, f32[64,64]{1,0:T(8,128...) custom-call(s32[272]{0:T(512)S(1)} %pad_add_fusion.slots_ref, ...), custom_call_target="tpu_custom_call" | custom-call | tf_op jit(solution)/shard_map/pallas_call | solution.py:338
  124.5 14.6 %all_to_all.22.terms_ref = bf16[8,2,64,128]{3,2,1,0:T(8,128)(2,1)S(1)} all-to-all(bf16[8,2,64,128]{3,2,1,0:T(8,128)(2,1)S(1)} %get-tuple-element.17), channel_id=1, replica_groups=mesh['rows'=8,'cols'=8,'seg'=4] {'cols'}, dimensions={0} | all-to-all | bytes 524288 | tf_op jit(solution)/shard_map/all_to_all | solution.py:459
  139.1 0.5 shard_map.113
  139.6 1.5 collective-permute-start.16
  141.2 0.5 collective-permute-start.15
  141.7 1.3 collective-permute-start.14
  143.0 0.9 collective-permute-done.16
  143.9 1.7 collective-permute-done.15
  145.6 0.0 collective-permute-done.14
  145.6 2.6 %collective-permute-start.19 = (f32[96,128]{1,0:T(8,128)S(1)}, f32[96,128]{1,0:T(8,128)S(1)}, u32[]{:S(2)}, u32[]{:S(2)}) collective-permute-start(f32[96,128]{1,0:T(8,128)S(1)} %add_add_fusion.1), channel_id=1, source_target_pairs={{0,192},{32,224},{64,128},{96,160},{128,64},{160,96},{192,0},{224,... | collective-permute-start | bytes 147464 | tf_op jit(solution)/shard_map/ppermute | solution.py:374
  148.2 0.6 collective-permute-start.18
  148.7 0.2 collective-permute-start.17
  149.0 0.9 collective-permute-done.19
  149.9 2.8 %collective-permute-done.18 = f32[96,128]{1,0:T(8,128)S(1)} collective-permute-done((f32[96,128]{1,0:T(8,128)S(1)}, f32[96,128]{1,0:T(8,128)S(1)}, u32[]{:S(2)}, u32[]{:S(2)}) %collective-permute-start.18) | collective-permute-done | bytes 49184 | tf_op jit(solution)/shard_map/ppermute | solution.py:374
  152.6 0.0 collective-permute-done.17
  152.6 4.7 %collective-permute-start.20 = (f32[96,128]{1,0:T(8,128)S(1)}, f32[96,128]{1,0:T(8,128)S(1)}, u32[]{:S(2)}, u32[]{:S(2)}) collective-permute-start(f32[96,128]{1,0:T(8,128)S(1)} %add_add_fusion), channel_id=1, source_target_pairs={{0,32},{32,0},{64,96},{96,64},{128,160},{160,128},{192,224},{224,1... | collective-permute-start | bytes 147464 | tf_op jit(solution)/shard_map/ppermute | solution.py:374
  157.4 0.9 collective-permute-done.20
  158.3 17.4 %all_to_all.23.grams_ref = f32[8,96,128]{2,1,0:T(8,128)S(1)} all-to-all(f32[8,96,128]{2,1,0:T(8,128)S(1)} %broadcast_in_dim.5), channel_id=1, replica_groups=mesh['rows'=8,'cols'=8,'seg'=4] {'cols'}, dimensions={0} | all-to-all | bytes 786432 | tf_op jit(solution)/shard_map/all_to_all | solution.py:397
  175.7 5.5 %shard_map.114 = (f32[64,2048]{1,0:T(8,128)}, f32[192,128]{1,0:T(8,128)}) custom-call(f32[8,96,128]{2,1,0:T(8,128)S(1)} %all_to_all.23.grams_ref, f32[64,64]{1,0:T(8,128)S(1)} %get-tuple-element.18.start_ref, f32[64,64]{1,0:T(8,128)S(1)} %get-tuple-element.19.head_ref, f32[64,64]{1,0:T(8,128)S(1)} %get-tuple-element.20.lower_ref, ...), custom_call_target="tpu_custom_call" | custom-call | tf_op jit(solution)/shard_map/pallas_call | solution.py:363
  (18 shorter events, 0.3 us)
Async XLA Ops:
  0.6 1.0 copy-start
  2.2 6.4 %collective-permute-start.2 = (f32[3,64,128]{2,1,0:T(8,128)S(1)}, f32[3,64,128]{2,1,0:T(8,128)S(1)}, u32[]{:S(2)}, u32[]{:S(2)}) collective-permute-start(f32[3,64,128]{2,1,0:T(8,128)S(1)} %shard_map.104.own_ref), channel_id=1, source_target_pairs={{0,3},{1,2},{2,1},{3,0},{4,7},{5,6},{6,5},{7,4},{8,11},{9,10},{10,... | collective-permute-start | bytes 294920 | tf_op jit(solution)/shard_map/ppermute | solution.py:374
  5.7 5.1 %collective-permute-start.1 = (f32[3,64,128]{2,1,0:T(8,128)S(1)}, f32[3,64,128]{2,1,0:T(8,128)S(1)}, u32[]{:S(2)}, u32[]{:S(2)}) collective-permute-start(f32[3,64,128]{2,1,0:T(8,128)S(1)} %shard_map.104.own_ref), channel_id=1, source_target_pairs={{0,2},{1,3},{2,0},{3,1},{4,6},{5,7},{6,4},{7,5},{8,10},{9,11},{10,... | collective-permute-start | bytes 294920 | tf_op jit(solution)/shard_map/ppermute | solution.py:374
  6.2 4.6 %collective-permute-start = (f32[3,64,128]{2,1,0:T(8,128)S(1)}, f32[3,64,128]{2,1,0:T(8,128)S(1)}, u32[]{:S(2)}, u32[]{:S(2)}) collective-permute-start(f32[3,64,128]{2,1,0:T(8,128)S(1)} %shard_map.104.own_ref), channel_id=1, source_target_pairs={{0,1},{1,0},{2,3},{3,2},{4,5},{5,4},{6,7},{7,6},{8,9},{9,8},{10,11... | collective-permute-start | bytes 294920 | tf_op jit(solution)/shard_map/ppermute | solution.py:374
  10.8 18.0 %copy-start.6 = (s32[1,1,1,16]{3,2,1,0:T(1,128)S(1)}, s32[1,1,1,16]{3,2,1,0:T(1,128)}, u32[]{:S(2)}) copy-start(s32[1,1,1,16]{3,2,1,0:T(1,128)} %param.12) | copy-start | bytes 196
  10.8 18.0 %copy-start.7 = (s32[1,1,1,16]{3,2,1,0:T(1,128)S(1)}, s32[1,1,1,16]{3,2,1,0:T(1,128)}, u32[]{:S(2)}) copy-start(s32[1,1,1,16]{3,2,1,0:T(1,128)} %param.11) | copy-start | bytes 196
  10.8 18.0 %copy-start.3 = (s32[1,1,1,256]{3,2,1,0:T(1,128)S(1)}, s32[1,1,1,256]{3,2,1,0:T(1,128)}, u32[]{:S(2)}) copy-start(s32[1,1,1,256]{3,2,1,0:T(1,128)} %param.16) | copy-start | bytes 3076
  10.8 18.0 %copy-start.4 = (s32[1,1,1,256]{3,2,1,0:T(1,128)S(1)}, s32[1,1,1,256]{3,2,1,0:T(1,128)}, u32[]{:S(2)}) copy-start(s32[1,1,1,256]{3,2,1,0:T(1,128)} %param.15) | copy-start | bytes 3076
  10.8 18.0 %copy-start.5 = (s32[1,1,1,256]{3,2,1,0:T(1,128)S(1)}, s32[1,1,1,256]{3,2,1,0:T(1,128)}, u32[]{:S(2)}) copy-start(s32[1,1,1,256]{3,2,1,0:T(1,128)} %param.17) | copy-start | bytes 3076
  10.8 20.2 %copy-start.2 = (bf16[1,1,1,16,128,128]{5,4,3,2,1,0:T(8,128)(2,1)S(1)}, bf16[1,1,1,16,128,128]{5,4,3,2,1,0:T(8,128)(2,1)}, u32[]{:S(2)}) copy-start(bf16[1,1,1,16,128,128]{5,4,3,2,1,0:T(8,128)(2,1)} %param.10) | copy-start | bytes 1572868
  10.8 15.3 %collective-permute-start.5 = (f32[9,64,128]{2,1,0:T(8,128)S(1)}, f32[9,64,128]{2,1,0:T(8,128)S(1)}, u32[]{:S(2)}, u32[]{:S(2)}) collective-permute-start(f32[9,64,128]{2,1,0:T(8,128)S(1)} %shard_map.105.own_ref), channel_id=1, source_target_pairs={{0,192},{32,224},{64,128},{96,160},{128,64},{160,96},{192,0},{224,... | collective-permute-start | bytes 884744 | tf_op jit(solution)/shard_map/ppermute | solution.py:374
  13.6 12.6 %collective-permute-start.4 = (f32[9,64,128]{2,1,0:T(8,128)S(1)}, f32[9,64,128]{2,1,0:T(8,128)S(1)}, u32[]{:S(2)}, u32[]{:S(2)}) collective-permute-start(f32[9,64,128]{2,1,0:T(8,128)S(1)} %shard_map.105.own_ref), channel_id=1, source_target_pairs={{0,128},{32,160},{64,192},{96,224},{128,0},{160,32},{192,64},{224,... | collective-permute-start | bytes 884744 | tf_op jit(solution)/shard_map/ppermute | solution.py:374
  13.9 12.2 %collective-permute-start.3 = (f32[9,64,128]{2,1,0:T(8,128)S(1)}, f32[9,64,128]{2,1,0:T(8,128)S(1)}, u32[]{:S(2)}, u32[]{:S(2)}) collective-permute-start(f32[9,64,128]{2,1,0:T(8,128)S(1)} %shard_map.105.own_ref), channel_id=1, source_target_pairs={{0,64},{32,96},{64,0},{96,32},{128,192},{160,224},{192,128},{224,1... | collective-permute-start | bytes 884744 | tf_op jit(solution)/shard_map/ppermute | solution.py:374
  26.2 4.8 %collective-permute-start.6 = (f32[33,64,128]{2,1,0:T(8,128)S(1)}, f32[33,64,128]{2,1,0:T(8,128)S(1)}, u32[]{:S(2)}, u32[]{:S(2)}) collective-permute-start(f32[33,64,128]{2,1,0:T(8,128)S(1)} %shard_map.106.refs_0_.refs_2_.refs_5_), channel_id=1, source_target_pairs={{0,32},{32,0},{64,96},{96,64},{128,160},{160,128},{192,224},{224,1... | collective-permute-start | bytes 3244040 | tf_op jit(solution)/shard_map/ppermute | solution.py:374
  65.9 17.2 %copy-start.1 = (f32[64,2048]{1,0:T(8,128)S(1)}, f32[64,2048]{1,0:T(8,128)}, u32[]{:S(2)}) copy-start(f32[64,2048]{1,0:T(8,128)} %right_ref.3) | copy-start | bytes 1572868
  84.6 5.4 %collective-permute-start.9 = (f32[3,64,128]{2,1,0:T(8,128)S(1)}, f32[3,64,128]{2,1,0:T(8,128)S(1)}, u32[]{:S(2)}, u32[]{:S(2)}) collective-permute-start(f32[3,64,128]{2,1,0:T(8,128)S(1)} %shard_map.109.own_ref), channel_id=1, source_target_pairs={{0,3},{1,2},{2,1},{3,0},{4,7},{5,6},{6,5},{7,4},{8,11},{9,10},{10,... | collective-permute-start | bytes 294920 | tf_op jit(solution)/shard_map/ppermute | solution.py:374
  87.4 5.0 %collective-permute-start.8 = (f32[3,64,128]{2,1,0:T(8,128)S(1)}, f32[3,64,128]{2,1,0:T(8,128)S(1)}, u32[]{:S(2)}, u32[]{:S(2)}) collective-permute-start(f32[3,64,128]{2,1,0:T(8,128)S(1)} %shard_map.109.own_ref), channel_id=1, source_target_pairs={{0,2},{1,3},{2,0},{3,1},{4,6},{5,7},{6,4},{7,5},{8,10},{9,11},{10,... | collective-permute-start | bytes 294920 | tf_op jit(solution)/shard_map/ppermute | solution.py:374
  87.7 4.7 %collective-permute-start.7 = (f32[3,64,128]{2,1,0:T(8,128)S(1)}, f32[3,64,128]{2,1,0:T(8,128)S(1)}, u32[]{:S(2)}, u32[]{:S(2)}) collective-permute-start(f32[3,64,128]{2,1,0:T(8,128)S(1)} %shard_map.109.own_ref), channel_id=1, source_target_pairs={{0,1},{1,0},{2,3},{3,2},{4,5},{5,4},{6,7},{7,6},{8,9},{9,8},{10,11... | collective-permute-start | bytes 294920 | tf_op jit(solution)/shard_map/ppermute | solution.py:374
  92.4 10.8 %collective-permute-start.12 = (f32[9,64,128]{2,1,0:T(8,128)S(1)}, f32[9,64,128]{2,1,0:T(8,128)S(1)}, u32[]{:S(2)}, u32[]{:S(2)}) collective-permute-start(f32[9,64,128]{2,1,0:T(8,128)S(1)} %shard_map.110.own_ref), channel_id=1, source_target_pairs={{0,192},{32,224},{64,128},{96,160},{128,64},{160,96},{192,0},{224,... | collective-permute-start | bytes 884744 | tf_op jit(solution)/shard_map/ppermute | solution.py:374
  94.7 8.5 %collective-permute-start.11 = (f32[9,64,128]{2,1,0:T(8,128)S(1)}, f32[9,64,128]{2,1,0:T(8,128)S(1)}, u32[]{:S(2)}, u32[]{:S(2)}) collective-permute-start(f32[9,64,128]{2,1,0:T(8,128)S(1)} %shard_map.110.own_ref), channel_id=1, source_target_pairs={{0,128},{32,160},{64,192},{96,224},{128,0},{160,32},{192,64},{224,... | collective-permute-start | bytes 884744 | tf_op jit(solution)/shard_map/ppermute | solution.py:374
  95.6 8.3 %collective-permute-start.10 = (f32[9,64,128]{2,1,0:T(8,128)S(1)}, f32[9,64,128]{2,1,0:T(8,128)S(1)}, u32[]{:S(2)}, u32[]{:S(2)}) collective-permute-start(f32[9,64,128]{2,1,0:T(8,128)S(1)} %shard_map.110.own_ref), channel_id=1, source_target_pairs={{0,64},{32,96},{64,0},{96,32},{128,192},{160,224},{192,128},{224,1... | collective-permute-start | bytes 884744 | tf_op jit(solution)/shard_map/ppermute | solution.py:374
  103.9 8.7 %collective-permute-start.13 = (f32[33,64,128]{2,1,0:T(8,128)S(1)}, f32[33,64,128]{2,1,0:T(8,128)S(1)}, u32[]{:S(2)}, u32[]{:S(2)}) collective-permute-start(f32[33,64,128]{2,1,0:T(8,128)S(1)} %shard_map.111.refs_0_.refs_3_), channel_id=1, source_target_pairs={{0,32},{32,0},{64,96},{96,64},{128,160},{160,128},{192,224},{224,1... | collective-permute-start | bytes 3244040 | tf_op jit(solution)/shard_map/ppermute | solution.py:374
  139.6 4.2 %collective-permute-start.16 = (f32[96,128]{1,0:T(8,128)S(1)}, f32[96,128]{1,0:T(8,128)S(1)}, u32[]{:S(2)}, u32[]{:S(2)}) collective-permute-start(f32[96,128]{1,0:T(8,128)S(1)} %shard_map.113), channel_id=1, source_target_pairs={{0,3},{1,2},{2,1},{3,0},{4,7},{5,6},{6,5},{7,4},{8,11},{9,10},{10,... | collective-permute-start | bytes 147464 | tf_op jit(solution)/shard_map/ppermute | solution.py:374
  141.2 4.5 %collective-permute-start.15 = (f32[96,128]{1,0:T(8,128)S(1)}, f32[96,128]{1,0:T(8,128)S(1)}, u32[]{:S(2)}, u32[]{:S(2)}) collective-permute-start(f32[96,128]{1,0:T(8,128)S(1)} %shard_map.113), channel_id=1, source_target_pairs={{0,2},{1,3},{2,0},{3,1},{4,6},{5,7},{6,4},{7,5},{8,10},{9,11},{10,... | collective-permute-start | bytes 147464 | tf_op jit(solution)/shard_map/ppermute | solution.py:374
  141.7 3.9 %collective-permute-start.14 = (f32[96,128]{1,0:T(8,128)S(1)}, f32[96,128]{1,0:T(8,128)S(1)}, u32[]{:S(2)}, u32[]{:S(2)}) collective-permute-start(f32[96,128]{1,0:T(8,128)S(1)} %shard_map.113), channel_id=1, source_target_pairs={{0,1},{1,0},{2,3},{3,2},{4,5},{5,4},{6,7},{7,6},{8,9},{9,8},{10,11... | collective-permute-start | bytes 147464 | tf_op jit(solution)/shard_map/ppermute | solution.py:374
  145.6 4.2 %collective-permute-start.19 = (f32[96,128]{1,0:T(8,128)S(1)}, f32[96,128]{1,0:T(8,128)S(1)}, u32[]{:S(2)}, u32[]{:S(2)}) collective-permute-start(f32[96,128]{1,0:T(8,128)S(1)} %add_add_fusion.1), channel_id=1, source_target_pairs={{0,192},{32,224},{64,128},{96,160},{128,64},{160,96},{192,0},{224,... | collective-permute-start | bytes 147464 | tf_op jit(solution)/shard_map/ppermute | solution.py:374
  148.2 4.4 %collective-permute-start.18 = (f32[96,128]{1,0:T(8,128)S(1)}, f32[96,128]{1,0:T(8,128)S(1)}, u32[]{:S(2)}, u32[]{:S(2)}) collective-permute-start(f32[96,128]{1,0:T(8,128)S(1)} %add_add_fusion.1), channel_id=1, source_target_pairs={{0,128},{32,160},{64,192},{96,224},{128,0},{160,32},{192,64},{224,... | collective-permute-start | bytes 147464 | tf_op jit(solution)/shard_map/ppermute | solution.py:374
  148.7 3.9 %collective-permute-start.17 = (f32[96,128]{1,0:T(8,128)S(1)}, f32[96,128]{1,0:T(8,128)S(1)}, u32[]{:S(2)}, u32[]{:S(2)}) collective-permute-start(f32[96,128]{1,0:T(8,128)S(1)} %add_add_fusion.1), channel_id=1, source_target_pairs={{0,64},{32,96},{64,0},{96,32},{128,192},{160,224},{192,128},{224,1... | collective-permute-start | bytes 147464 | tf_op jit(solution)/shard_map/ppermute | solution.py:374
  152.6 5.6 %collective-permute-start.20 = (f32[96,128]{1,0:T(8,128)S(1)}, f32[96,128]{1,0:T(8,128)S(1)}, u32[]{:S(2)}, u32[]{:S(2)}) collective-permute-start(f32[96,128]{1,0:T(8,128)S(1)} %add_add_fusion), channel_id=1, source_target_pairs={{0,32},{32,0},{64,96},{96,64},{128,160},{160,128},{192,224},{224,1... | collective-permute-start | bytes 147464 | tf_op jit(solution)/shard_map/ppermute | solution.py:374

commit v4 on v3

--- a/solution.py
+++ b/solution.py
@@ -121,8 +121,11 @@
     return jnp.concatenate(parts, 1)
 
 
-def sum_kernel(terms_ref, share_ref):
-    share_ref[...] = sum_leading(terms_ref)
+def sum_kernel(terms_ref, share_ref, spread_ref):
+    total = sum_leading(terms_ref)
+    share_ref[...] = total
+    for at in range(spread_ref.shape[0]):
+        spread_ref[at] = total
 
 
 def first_image_kernel(base_ref, right_ref, image_ref, share_ref, message_ref):
@@ -280,7 +283,7 @@
             rounded[side * half_count + index] = value.astype(jnp.bfloat16)
             return 0
 
-        lax.fori_loop(0, half_count, make_basis, 0, unroll=8)
+        lax.fori_loop(0, half_count, make_basis, 0, unroll=32)
 
     order = rounded.shape[1]
     columns = lax.broadcasted_iota(jnp.int32, (order, left.shape[1]), 1)
@@ -292,8 +295,8 @@
 
     def near_step(step, _):
         values = []
-        for inner in range(4):
-            at = step * 4 + inner
+        for inner in range(16):
+            at = step * 16 + inner
             row, column = row_and_column(slots_ref[slots + at])
             value = lax.dot_general(rounded[column], near[at], NT, preferred_element_type=jnp.float32)
             values.append((row, value))
@@ -301,7 +304,7 @@
             total[row // group, row % group] += value
         return 0
 
-    lax.fori_loop(0, near.shape[0] // 4, near_step, 0)
+    lax.fori_loop(0, near.shape[0] // 16, near_step, 0)
 
     def slot_step(step, _):
         coefs = []
@@ -443,8 +446,8 @@
         start_mixes, 2, start_halves, start_halves, operator, terms_shape, jnp.float32
     )
     received = lax.all_to_all(terms, "cols", 0, 0)
-    (share,) = call(sum_kernel, [share_shape], received)
-    image_piece = spread_cols(share)
+    share, spread = call(sum_kernel, [share_shape, terms_shape], received)
+    image_piece = lax.all_to_all(spread, "cols", 0, 0)
     (message,) = call(first_image_kernel, [message_shape], base, right_side, image_piece, share)
     image_halves = gather_halves(message)
     head, lower, top_inverse, own, mix, second_share, terms = apply_operator(

time: 181 us -> 181 us (level)
    all_to_all x0 -> x1, blocking collectives: none -> 17 us  [body(): image_piece = lax.all_to_all(spread, 'cols', 0, 0)]
    all_to_all x2 -> x1, blocking collectives: 34.5 us -> 17.6 us  [spread_cols(): lax.all_to_all(jnp.broadcast_to(values[None], (count,) + values.shape), '...]
where the time goes in v4:
time: 181 us; the launch traced here: 180 us
  blocking collectives  74 us (41%)
  waiting for transfers between devices  40.4 us (22%)
  starting transfers between devices  34.6 us (19%)
  Pallas kernels  29.4 us (16%)
    ppermute x21, waiting for transfers between devices, exchange(): lax.ppermute(values, axis, [(at, at ^ distance) for at in range(count)])  40.4 us
    all_to_all x2, blocking collectives, body(): received = lax.all_to_all(terms, 'cols', 0, 0)  39.4 us
    ppermute x21, starting transfers between devices, exchange(): lax.ppermute(values, axis, [(at, at ^ distance) for at in range(count)])  34.6 us
    pallas_call x2, Pallas kernels, apply_operator(): pl.pallas_call(functools.partial(apply_kernel, prepare, len(grams), small...  21.1 us
    all_to_all x1, blocking collectives, spread_cols(): lax.all_to_all(jnp.broadcast_to(values[None], (count,) + values.shape), '...  17.6 us
    all_to_all x1, blocking collectives, body(): image_piece = lax.all_to_all(spread, 'cols', 0, 0)  17 us
    pallas_call x9, Pallas kernels, call(): pl.pallas_call(kernel, out_shape=tuple((jax.ShapeDtypeStruct(shape, jnp.f...  8.36 us
  transfers between devices with their start and end apart: 21, of which 14 were waited for; matrix products, arithmetic and copies ran while one was open for 0% of the time, Pallas kernels for 0%

profile of v4, /device:TPU:1, one launch (start us, length us, event | category | flops | bytes accessed | tf_op | source)
XLA Modules:
  0.0 180.5 jit_solution(12716435437734740588)
XLA Ops:
  0.6 0.0 copy-start
  0.6 1.0 copy-done
  1.7 0.6 shard_map.104.own_ref
  2.2 3.4 %collective-permute-start.2 = (f32[3,64,128]{2,1,0:T(8,128)S(1)}, f32[3,64,128]{2,1,0:T(8,128)S(1)}, u32[]{:S(2)}, u32[]{:S(2)}) collective-permute-start(f32[3,64,128]{2,1,0:T(8,128)S(1)} %shard_map.104.own_ref), channel_id=1, source_target_pairs={{0,3},{1,2},{2,1},{3,0},{4,7},{5,6},{6,5},{7,4},{8,11},{9,10},{10,... | collective-permute-start | bytes 294920 | tf_op jit(solution)/shard_map/ppermute | solution.py:377
  5.7 0.5 collective-permute-start.1
  6.2 0.2 collective-permute-start
  6.3 2.3 %collective-permute-done.2.three_ref = f32[3,64,128]{2,1,0:T(8,128)S(1)} collective-permute-done((f32[3,64,128]{2,1,0:T(8,128)S(1)}, f32[3,64,128]{2,1,0:T(8,128)S(1)}, u32[]{:S(2)}, u32[]{:S(2)}) %collective-permute-start.2) | collective-permute-done | bytes 98336 | tf_op jit(solution)/shard_map/ppermute | solution.py:377
  8.7 2.1 %collective-permute-done.1.two_ref = f32[3,64,128]{2,1,0:T(8,128)S(1)} collective-permute-done((f32[3,64,128]{2,1,0:T(8,128)S(1)}, f32[3,64,128]{2,1,0:T(8,128)S(1)}, u32[]{:S(2)}, u32[]{:S(2)}) %collective-permute-start.1) | collective-permute-done | bytes 98336 | tf_op jit(solution)/shard_map/ppermute | solution.py:377
  10.7 0.0 collective-permute-done.one_ref
  10.8 0.0 copy-start.6
  10.8 0.0 copy-start.7
  10.8 0.0 copy-start.3
  10.8 0.0 copy-start.4
  10.8 0.0 copy-start.5
  10.8 0.0 copy-start.2
  10.8 2.7 %collective-permute-start.5 = (f32[9,64,128]{2,1,0:T(8,128)S(1)}, f32[9,64,128]{2,1,0:T(8,128)S(1)}, u32[]{:S(2)}, u32[]{:S(2)}) collective-permute-start(f32[9,64,128]{2,1,0:T(8,128)S(1)} %shard_map.105.own_ref), channel_id=1, source_target_pairs={{0,192},{32,224},{64,128},{96,160},{128,64},{160,96},{192,0},{224,... | collective-permute-start | bytes 884744 | tf_op jit(solution)/shard_map/ppermute | solution.py:377
  13.6 0.3 collective-permute-start.4
  13.9 0.3 collective-permute-start.3
  14.2 11.9 %collective-permute-done.5.three_ref = f32[9,64,128]{2,1,0:T(8,128)S(1)} collective-permute-done((f32[9,64,128]{2,1,0:T(8,128)S(1)}, f32[9,64,128]{2,1,0:T(8,128)S(1)}, u32[]{:S(2)}, u32[]{:S(2)}) %collective-permute-start.5) | collective-permute-done | bytes 294944 | tf_op jit(solution)/shard_map/ppermute | solution.py:377
  26.1 0.0 collective-permute-done.4.two_ref
  26.1 0.0 collective-permute-done.3.one_ref
  26.1 0.1 shard_map.106.refs_0_.refs_2_.refs_5_
  26.2 2.5 %collective-permute-start.6 = (f32[33,64,128]{2,1,0:T(8,128)S(1)}, f32[33,64,128]{2,1,0:T(8,128)S(1)}, u32[]{:S(2)}, u32[]{:S(2)}) collective-permute-start(f32[33,64,128]{2,1,0:T(8,128)S(1)} %shard_map.106.refs_0_.refs_2_.refs_5_), channel_id=1, source_target_pairs={{0,32},{32,0},{64,96},{96,64},{128,160},{160,128},{192,224},{224,1... | collective-permute-start | bytes 3244040 | tf_op jit(solution)/shard_map/ppermute | solution.py:377
  28.7 0.0 copy-done.3
  28.8 2.2 %collective-permute-done.6.refs_1_.refs_3_.refs_6_ = f32[33,64,128]{2,1,0:T(8,128)S(1)} collective-permute-done((f32[33,64,128]{2,1,0:T(8,128)S(1)}, f32[33,64,128]{2,1,0:T(8,128)S(1)}, u32[]{:S(2)}, u32[]{:S(2)}) %collective-permute-start.6) | collective-permute-done | bytes 1081376 | tf_op jit(solution)/shard_map/ppermute | solution.py:377
  31.1 10.0 %shard_map.107 = (f32[64,64]{1,0:T(8,128)S(1)}, f32[64,64]{1,0:T(8,128)S(1)}, f32[2,64,128]{2,1,0:T(8,128)S(1)}, f32[8,2,64,128]{3,2,1,0:T(8,128)S(1)}) custom-call(s32[272]{0:T(512)S(1)} %pad_add_fusion.slots_ref, f32[33,64,128]{2,1,0:T(8,128)S(1)} %shard_map.106.refs_0_.refs_2_.refs_5_, f32[33,64,128]{2,1,0:T(8,128)S(1)} %collective-permute-done.6.refs_1_.refs_3_.refs_6_, ...), custom_call_target="tpu_custom_call" | custom-call | tf_op jit(solution)/shard_map/pallas_call | solution.py:341
  41.0 0.0 copy-start.1
  41.0 24.7 %all_to_all.20.terms_ref = f32[8,2,64,128]{3,2,1,0:T(8,128)S(1)} all-to-all(f32[8,2,64,128]{3,2,1,0:T(8,128)S(1)} %get-tuple-element.17), channel_id=1, replica_groups=mesh['rows'=8,'cols'=8,'seg'=4] {'cols'}, dimensions={0} | all-to-all | bytes 1048576 | tf_op jit(solution)/shard_map/all_to_all | solution.py:448
  65.8 17.0 %all_to_all.21.image_ref = f32[8,2,64,128]{3,2,1,0:T(8,128)S(1)} all-to-all(f32[8,2,64,128]{3,2,1,0:T(8,128)S(1)} %get-tuple-element.18), channel_id=1, replica_groups=mesh['rows'=8,'cols'=8,'seg'=4] {'cols'}, dimensions={0} | all-to-all | bytes 1048576 | tf_op jit(solution)/shard_map/all_to_all | solution.py:450
  82.9 1.5 shard_map.109.own_ref
  84.3 2.6 %collective-permute-start.9 = (f32[3,64,128]{2,1,0:T(8,128)S(1)}, f32[3,64,128]{2,1,0:T(8,128)S(1)}, u32[]{:S(2)}, u32[]{:S(2)}) collective-permute-start(f32[3,64,128]{2,1,0:T(8,128)S(1)} %shard_map.109.own_ref), channel_id=1, source_target_pairs={{0,3},{1,2},{2,1},{3,0},{4,7},{5,6},{6,5},{7,4},{8,11},{9,10},{10,... | collective-permute-start | bytes 294920 | tf_op jit(solution)/shard_map/ppermute | solution.py:377
  87.0 0.8 collective-permute-start.8
  87.8 0.0 collective-permute-start.7
  87.8 1.8 %collective-permute-done.9.three_ref = f32[3,64,128]{2,1,0:T(8,128)S(1)} collective-permute-done((f32[3,64,128]{2,1,0:T(8,128)S(1)}, f32[3,64,128]{2,1,0:T(8,128)S(1)}, u32[]{:S(2)}, u32[]{:S(2)}) %collective-permute-start.9) | collective-permute-done | bytes 98336 | tf_op jit(solution)/shard_map/ppermute | solution.py:377
  89.6 2.4 %collective-permute-done.8.two_ref = f32[3,64,128]{2,1,0:T(8,128)S(1)} collective-permute-done((f32[3,64,128]{2,1,0:T(8,128)S(1)}, f32[3,64,128]{2,1,0:T(8,128)S(1)}, u32[]{:S(2)}, u32[]{:S(2)}) %collective-permute-start.8) | collective-permute-done | bytes 98336 | tf_op jit(solution)/shard_map/ppermute | solution.py:377
  92.0 0.0 collective-permute-done.7.one_ref
  92.0 2.3 %collective-permute-start.12 = (f32[9,64,128]{2,1,0:T(8,128)S(1)}, f32[9,64,128]{2,1,0:T(8,128)S(1)}, u32[]{:S(2)}, u32[]{:S(2)}) collective-permute-start(f32[9,64,128]{2,1,0:T(8,128)S(1)} %shard_map.110.own_ref), channel_id=1, source_target_pairs={{0,192},{32,224},{64,128},{96,160},{128,64},{160,96},{192,0},{224,... | collective-permute-start | bytes 884744 | tf_op jit(solution)/shard_map/ppermute | solution.py:377
  94.3 0.7 collective-permute-start.11
  95.0 0.4 collective-permute-start.10
  95.3 7.5 %collective-permute-done.12.three_ref = f32[9,64,128]{2,1,0:T(8,128)S(1)} collective-permute-done((f32[9,64,128]{2,1,0:T(8,128)S(1)}, f32[9,64,128]{2,1,0:T(8,128)S(1)}, u32[]{:S(2)}, u32[]{:S(2)}) %collective-permute-start.12) | collective-permute-done | bytes 294944 | tf_op jit(solution)/shard_map/ppermute | solution.py:377
  102.8 0.0 collective-permute-done.11.two_ref
  102.8 0.6 collective-permute-done.10.one_ref
  103.4 0.1 shard_map.111.refs_0_.refs_3_
  103.5 6.4 %collective-permute-start.13 = (f32[33,64,128]{2,1,0:T(8,128)S(1)}, f32[33,64,128]{2,1,0:T(8,128)S(1)}, u32[]{:S(2)}, u32[]{:S(2)}) collective-permute-start(f32[33,64,128]{2,1,0:T(8,128)S(1)} %shard_map.111.refs_0_.refs_3_), channel_id=1, source_target_pairs={{0,32},{32,0},{64,96},{96,64},{128,160},{160,128},{192,224},{224,1... | collective-permute-start | bytes 3244040 | tf_op jit(solution)/shard_map/ppermute | solution.py:377
  109.9 2.3 %collective-permute-done.13.refs_1_.refs_4_ = f32[33,64,128]{2,1,0:T(8,128)S(1)} collective-permute-done((f32[33,64,128]{2,1,0:T(8,128)S(1)}, f32[33,64,128]{2,1,0:T(8,128)S(1)}, u32[]{:S(2)}, u32[]{:S(2)}) %collective-permute-start.13) | collective-permute-done | bytes 1081376 | tf_op jit(solution)/shard_map/ppermute | solution.py:377
  112.2 11.1 %shard_map.112 = (f32[64,64]{1,0:T(8,128)S(1)}, f32[64,64]{1,0:T(8,128)S(1)}, f32[64,64]{1,0:T(8,128)S(1)}, f32[64,64]{1,0:T(8,128)S(1)}, f32[64,64]{1,0:T(8,128...) custom-call(s32[272]{0:T(512)S(1)} %pad_add_fusion.slots_ref, ...), custom_call_target="tpu_custom_call" | custom-call | tf_op jit(solution)/shard_map/pallas_call | solution.py:341
  123.3 14.7 %all_to_all.22.terms_ref = bf16[8,2,64,128]{3,2,1,0:T(8,128)(2,1)S(1)} all-to-all(bf16[8,2,64,128]{3,2,1,0:T(8,128)(2,1)S(1)} %get-tuple-element.21), channel_id=1, replica_groups=mesh['rows'=8,'cols'=8,'seg'=4] {'cols'}, dimensions={0} | all-to-all | bytes 524288 | tf_op jit(solution)/shard_map/all_to_all | solution.py:462
  138.0 0.5 shard_map.113
  138.5 1.6 collective-permute-start.16
  140.1 0.5 collective-permute-start.15
  140.6 1.2 collective-permute-start.14
  141.8 0.9 collective-permute-done.16
  142.7 1.9 %collective-permute-done.15 = f32[96,128]{1,0:T(8,128)S(1)} collective-permute-done((f32[96,128]{1,0:T(8,128)S(1)}, f32[96,128]{1,0:T(8,128)S(1)}, u32[]{:S(2)}, u32[]{:S(2)}) %collective-permute-start.15) | collective-permute-done | bytes 49184 | tf_op jit(solution)/shard_map/ppermute | solution.py:377
  144.6 0.0 collective-permute-done.14
  144.6 2.5 %collective-permute-start.19 = (f32[96,128]{1,0:T(8,128)S(1)}, f32[96,128]{1,0:T(8,128)S(1)}, u32[]{:S(2)}, u32[]{:S(2)}) collective-permute-start(f32[96,128]{1,0:T(8,128)S(1)} %add_add_fusion.1), channel_id=1, source_target_pairs={{0,192},{32,224},{64,128},{96,160},{128,64},{160,96},{192,0},{224,... | collective-permute-start | bytes 147464 | tf_op jit(solution)/shard_map/ppermute | solution.py:377
  147.1 0.5 collective-permute-start.18
  147.6 0.3 collective-permute-start.17
  148.0 0.9 collective-permute-done.19
  148.9 2.7 %collective-permute-done.18 = f32[96,128]{1,0:T(8,128)S(1)} collective-permute-done((f32[96,128]{1,0:T(8,128)S(1)}, f32[96,128]{1,0:T(8,128)S(1)}, u32[]{:S(2)}, u32[]{:S(2)}) %collective-permute-start.18) | collective-permute-done | bytes 49184 | tf_op jit(solution)/shard_map/ppermute | solution.py:377
  151.6 0.0 collective-permute-done.17
  151.6 4.9 %collective-permute-start.20 = (f32[96,128]{1,0:T(8,128)S(1)}, f32[96,128]{1,0:T(8,128)S(1)}, u32[]{:S(2)}, u32[]{:S(2)}) collective-permute-start(f32[96,128]{1,0:T(8,128)S(1)} %add_add_fusion), channel_id=1, source_target_pairs={{0,32},{32,0},{64,96},{96,64},{128,160},{160,128},{192,224},{224,1... | collective-permute-start | bytes 147464 | tf_op jit(solution)/shard_map/ppermute | solution.py:377
  156.5 0.9 collective-permute-done.20
  157.4 17.6 %all_to_all.23.grams_ref = f32[8,96,128]{2,1,0:T(8,128)S(1)} all-to-all(f32[8,96,128]{2,1,0:T(8,128)S(1)} %broadcast_in_dim.2), channel_id=1, replica_groups=mesh['rows'=8,'cols'=8,'seg'=4] {'cols'}, dimensions={0} | all-to-all | bytes 786432 | tf_op jit(solution)/shard_map/all_to_all | solution.py:400
  174.9 5.5 %shard_map.114 = (f32[64,2048]{1,0:T(8,128)}, f32[192,128]{1,0:T(8,128)}) custom-call(f32[8,96,128]{2,1,0:T(8,128)S(1)} %all_to_all.23.grams_ref, f32[64,64]{1,0:T(8,128)S(1)} %get-tuple-element.22.start_ref, f32[64,64]{1,0:T(8,128)S(1)} %get-tuple-element.23.head_ref, f32[64,64]{1,0:T(8,128)S(1)} %get-tuple-element.24.lower_ref, ...), custom_call_target="tpu_custom_call" | custom-call | tf_op jit(solution)/shard_map/pallas_call | solution.py:366
  (17 shorter events, 0.2 us)
Async XLA Ops:
  0.6 1.0 copy-start
  2.2 6.4 %collective-permute-start.2 = (f32[3,64,128]{2,1,0:T(8,128)S(1)}, f32[3,64,128]{2,1,0:T(8,128)S(1)}, u32[]{:S(2)}, u32[]{:S(2)}) collective-permute-start(f32[3,64,128]{2,1,0:T(8,128)S(1)} %shard_map.104.own_ref), channel_id=1, source_target_pairs={{0,3},{1,2},{2,1},{3,0},{4,7},{5,6},{6,5},{7,4},{8,11},{9,10},{10,... | collective-permute-start | bytes 294920 | tf_op jit(solution)/shard_map/ppermute | solution.py:377
  5.7 5.1 %collective-permute-start.1 = (f32[3,64,128]{2,1,0:T(8,128)S(1)}, f32[3,64,128]{2,1,0:T(8,128)S(1)}, u32[]{:S(2)}, u32[]{:S(2)}) collective-permute-start(f32[3,64,128]{2,1,0:T(8,128)S(1)} %shard_map.104.own_ref), channel_id=1, source_target_pairs={{0,2},{1,3},{2,0},{3,1},{4,6},{5,7},{6,4},{7,5},{8,10},{9,11},{10,... | collective-permute-start | bytes 294920 | tf_op jit(solution)/shard_map/ppermute | solution.py:377
  6.2 4.6 %collective-permute-start = (f32[3,64,128]{2,1,0:T(8,128)S(1)}, f32[3,64,128]{2,1,0:T(8,128)S(1)}, u32[]{:S(2)}, u32[]{:S(2)}) collective-permute-start(f32[3,64,128]{2,1,0:T(8,128)S(1)} %shard_map.104.own_ref), channel_id=1, source_target_pairs={{0,1},{1,0},{2,3},{3,2},{4,5},{5,4},{6,7},{7,6},{8,9},{9,8},{10,11... | collective-permute-start | bytes 294920 | tf_op jit(solution)/shard_map/ppermute | solution.py:377
  10.8 18.0 %copy-start.6 = (s32[1,1,1,16]{3,2,1,0:T(1,128)S(1)}, s32[1,1,1,16]{3,2,1,0:T(1,128)}, u32[]{:S(2)}) copy-start(s32[1,1,1,16]{3,2,1,0:T(1,128)} %param.12) | copy-start | bytes 196
  10.8 18.0 %copy-start.7 = (s32[1,1,1,16]{3,2,1,0:T(1,128)S(1)}, s32[1,1,1,16]{3,2,1,0:T(1,128)}, u32[]{:S(2)}) copy-start(s32[1,1,1,16]{3,2,1,0:T(1,128)} %param.11) | copy-start | bytes 196
  10.8 18.0 %copy-start.3 = (s32[1,1,1,256]{3,2,1,0:T(1,128)S(1)}, s32[1,1,1,256]{3,2,1,0:T(1,128)}, u32[]{:S(2)}) copy-start(s32[1,1,1,256]{3,2,1,0:T(1,128)} %param.16) | copy-start | bytes 3076
  10.8 18.0 %copy-start.4 = (s32[1,1,1,256]{3,2,1,0:T(1,128)S(1)}, s32[1,1,1,256]{3,2,1,0:T(1,128)}, u32[]{:S(2)}) copy-start(s32[1,1,1,256]{3,2,1,0:T(1,128)} %param.15) | copy-start | bytes 3076
  10.8 18.0 %copy-start.5 = (s32[1,1,1,256]{3,2,1,0:T(1,128)S(1)}, s32[1,1,1,256]{3,2,1,0:T(1,128)}, u32[]{:S(2)}) copy-start(s32[1,1,1,256]{3,2,1,0:T(1,128)} %param.17) | copy-start | bytes 3076
  10.8 20.2 %copy-start.2 = (bf16[1,1,1,16,128,128]{5,4,3,2,1,0:T(8,128)(2,1)S(1)}, bf16[1,1,1,16,128,128]{5,4,3,2,1,0:T(8,128)(2,1)}, u32[]{:S(2)}) copy-start(bf16[1,1,1,16,128,128]{5,4,3,2,1,0:T(8,128)(2,1)} %param.10) | copy-start | bytes 1572868
  10.8 15.3 %collective-permute-start.5 = (f32[9,64,128]{2,1,0:T(8,128)S(1)}, f32[9,64,128]{2,1,0:T(8,128)S(1)}, u32[]{:S(2)}, u32[]{:S(2)}) collective-permute-start(f32[9,64,128]{2,1,0:T(8,128)S(1)} %shard_map.105.own_ref), channel_id=1, source_target_pairs={{0,192},{32,224},{64,128},{96,160},{128,64},{160,96},{192,0},{224,... | collective-permute-start | bytes 884744 | tf_op jit(solution)/shard_map/ppermute | solution.py:377
  13.6 12.6 %collective-permute-start.4 = (f32[9,64,128]{2,1,0:T(8,128)S(1)}, f32[9,64,128]{2,1,0:T(8,128)S(1)}, u32[]{:S(2)}, u32[]{:S(2)}) collective-permute-start(f32[9,64,128]{2,1,0:T(8,128)S(1)} %shard_map.105.own_ref), channel_id=1, source_target_pairs={{0,128},{32,160},{64,192},{96,224},{128,0},{160,32},{192,64},{224,... | collective-permute-start | bytes 884744 | tf_op jit(solution)/shard_map/ppermute | solution.py:377
  13.9 12.2 %collective-permute-start.3 = (f32[9,64,128]{2,1,0:T(8,128)S(1)}, f32[9,64,128]{2,1,0:T(8,128)S(1)}, u32[]{:S(2)}, u32[]{:S(2)}) collective-permute-start(f32[9,64,128]{2,1,0:T(8,128)S(1)} %shard_map.105.own_ref), channel_id=1, source_target_pairs={{0,64},{32,96},{64,0},{96,32},{128,192},{160,224},{192,128},{224,1... | collective-permute-start | bytes 884744 | tf_op jit(solution)/shard_map/ppermute | solution.py:377
  26.2 4.8 %collective-permute-start.6 = (f32[33,64,128]{2,1,0:T(8,128)S(1)}, f32[33,64,128]{2,1,0:T(8,128)S(1)}, u32[]{:S(2)}, u32[]{:S(2)}) collective-permute-start(f32[33,64,128]{2,1,0:T(8,128)S(1)} %shard_map.106.refs_0_.refs_2_.refs_5_), channel_id=1, source_target_pairs={{0,32},{32,0},{64,96},{96,64},{128,160},{160,128},{192,224},{224,1... | collective-permute-start | bytes 3244040 | tf_op jit(solution)/shard_map/ppermute | solution.py:377
  41.0 41.8 %copy-start.1 = (f32[64,2048]{1,0:T(8,128)S(1)}, f32[64,2048]{1,0:T(8,128)}, u32[]{:S(2)}) copy-start(f32[64,2048]{1,0:T(8,128)} %right_ref.3) | copy-start | bytes 1572868
  84.3 5.3 %collective-permute-start.9 = (f32[3,64,128]{2,1,0:T(8,128)S(1)}, f32[3,64,128]{2,1,0:T(8,128)S(1)}, u32[]{:S(2)}, u32[]{:S(2)}) collective-permute-start(f32[3,64,128]{2,1,0:T(8,128)S(1)} %shard_map.109.own_ref), channel_id=1, source_target_pairs={{0,3},{1,2},{2,1},{3,0},{4,7},{5,6},{6,5},{7,4},{8,11},{9,10},{10,... | collective-permute-start | bytes 294920 | tf_op jit(solution)/shard_map/ppermute | solution.py:377
  87.0 5.0 %collective-permute-start.8 = (f32[3,64,128]{2,1,0:T(8,128)S(1)}, f32[3,64,128]{2,1,0:T(8,128)S(1)}, u32[]{:S(2)}, u32[]{:S(2)}) collective-permute-start(f32[3,64,128]{2,1,0:T(8,128)S(1)} %shard_map.109.own_ref), channel_id=1, source_target_pairs={{0,2},{1,3},{2,0},{3,1},{4,6},{5,7},{6,4},{7,5},{8,10},{9,11},{10,... | collective-permute-start | bytes 294920 | tf_op jit(solution)/shard_map/ppermute | solution.py:377
  87.8 4.2 %collective-permute-start.7 = (f32[3,64,128]{2,1,0:T(8,128)S(1)}, f32[3,64,128]{2,1,0:T(8,128)S(1)}, u32[]{:S(2)}, u32[]{:S(2)}) collective-permute-start(f32[3,64,128]{2,1,0:T(8,128)S(1)} %shard_map.109.own_ref), channel_id=1, source_target_pairs={{0,1},{1,0},{2,3},{3,2},{4,5},{5,4},{6,7},{7,6},{8,9},{9,8},{10,11... | collective-permute-start | bytes 294920 | tf_op jit(solution)/shard_map/ppermute | solution.py:377
  92.0 10.8 %collective-permute-start.12 = (f32[9,64,128]{2,1,0:T(8,128)S(1)}, f32[9,64,128]{2,1,0:T(8,128)S(1)}, u32[]{:S(2)}, u32[]{:S(2)}) collective-permute-start(f32[9,64,128]{2,1,0:T(8,128)S(1)} %shard_map.110.own_ref), channel_id=1, source_target_pairs={{0,192},{32,224},{64,128},{96,160},{128,64},{160,96},{192,0},{224,... | collective-permute-start | bytes 884744 | tf_op jit(solution)/shard_map/ppermute | solution.py:377
  94.3 8.5 %collective-permute-start.11 = (f32[9,64,128]{2,1,0:T(8,128)S(1)}, f32[9,64,128]{2,1,0:T(8,128)S(1)}, u32[]{:S(2)}, u32[]{:S(2)}) collective-permute-start(f32[9,64,128]{2,1,0:T(8,128)S(1)} %shard_map.110.own_ref), channel_id=1, source_target_pairs={{0,128},{32,160},{64,192},{96,224},{128,0},{160,32},{192,64},{224,... | collective-permute-start | bytes 884744 | tf_op jit(solution)/shard_map/ppermute | solution.py:377
  95.0 8.5 %collective-permute-start.10 = (f32[9,64,128]{2,1,0:T(8,128)S(1)}, f32[9,64,128]{2,1,0:T(8,128)S(1)}, u32[]{:S(2)}, u32[]{:S(2)}) collective-permute-start(f32[9,64,128]{2,1,0:T(8,128)S(1)} %shard_map.110.own_ref), channel_id=1, source_target_pairs={{0,64},{32,96},{64,0},{96,32},{128,192},{160,224},{192,128},{224,1... | collective-permute-start | bytes 884744 | tf_op jit(solution)/shard_map/ppermute | solution.py:377
  103.5 8.7 %collective-permute-start.13 = (f32[33,64,128]{2,1,0:T(8,128)S(1)}, f32[33,64,128]{2,1,0:T(8,128)S(1)}, u32[]{:S(2)}, u32[]{:S(2)}) collective-permute-start(f32[33,64,128]{2,1,0:T(8,128)S(1)} %shard_map.111.refs_0_.refs_3_), channel_id=1, source_target_pairs={{0,32},{32,0},{64,96},{96,64},{128,160},{160,128},{192,224},{224,1... | collective-permute-start | bytes 3244040 | tf_op jit(solution)/shard_map/ppermute | solution.py:377
  138.5 4.2 %collective-permute-start.16 = (f32[96,128]{1,0:T(8,128)S(1)}, f32[96,128]{1,0:T(8,128)S(1)}, u32[]{:S(2)}, u32[]{:S(2)}) collective-permute-start(f32[96,128]{1,0:T(8,128)S(1)} %shard_map.113), channel_id=1, source_target_pairs={{0,3},{1,2},{2,1},{3,0},{4,7},{5,6},{6,5},{7,4},{8,11},{9,10},{10,... | collective-permute-start | bytes 147464 | tf_op jit(solution)/shard_map/ppermute | solution.py:377
  140.1 4.5 %collective-permute-start.15 = (f32[96,128]{1,0:T(8,128)S(1)}, f32[96,128]{1,0:T(8,128)S(1)}, u32[]{:S(2)}, u32[]{:S(2)}) collective-permute-start(f32[96,128]{1,0:T(8,128)S(1)} %shard_map.113), channel_id=1, source_target_pairs={{0,2},{1,3},{2,0},{3,1},{4,6},{5,7},{6,4},{7,5},{8,10},{9,11},{10,... | collective-permute-start | bytes 147464 | tf_op jit(solution)/shard_map/ppermute | solution.py:377
  140.6 4.0 %collective-permute-start.14 = (f32[96,128]{1,0:T(8,128)S(1)}, f32[96,128]{1,0:T(8,128)S(1)}, u32[]{:S(2)}, u32[]{:S(2)}) collective-permute-start(f32[96,128]{1,0:T(8,128)S(1)} %shard_map.113), channel_id=1, source_target_pairs={{0,1},{1,0},{2,3},{3,2},{4,5},{5,4},{6,7},{7,6},{8,9},{9,8},{10,11... | collective-permute-start | bytes 147464 | tf_op jit(solution)/shard_map/ppermute | solution.py:377
  144.6 4.2 %collective-permute-start.19 = (f32[96,128]{1,0:T(8,128)S(1)}, f32[96,128]{1,0:T(8,128)S(1)}, u32[]{:S(2)}, u32[]{:S(2)}) collective-permute-start(f32[96,128]{1,0:T(8,128)S(1)} %add_add_fusion.1), channel_id=1, source_target_pairs={{0,192},{32,224},{64,128},{96,160},{128,64},{160,96},{192,0},{224,... | collective-permute-start | bytes 147464 | tf_op jit(solution)/shard_map/ppermute | solution.py:377
  147.1 4.4 %collective-permute-start.18 = (f32[96,128]{1,0:T(8,128)S(1)}, f32[96,128]{1,0:T(8,128)S(1)}, u32[]{:S(2)}, u32[]{:S(2)}) collective-permute-start(f32[96,128]{1,0:T(8,128)S(1)} %add_add_fusion.1), channel_id=1, source_target_pairs={{0,128},{32,160},{64,192},{96,224},{128,0},{160,32},{192,64},{224,... | collective-permute-start | bytes 147464 | tf_op jit(solution)/shard_map/ppermute | solution.py:377
  147.6 4.0 %collective-permute-start.17 = (f32[96,128]{1,0:T(8,128)S(1)}, f32[96,128]{1,0:T(8,128)S(1)}, u32[]{:S(2)}, u32[]{:S(2)}) collective-permute-start(f32[96,128]{1,0:T(8,128)S(1)} %add_add_fusion.1), channel_id=1, source_target_pairs={{0,64},{32,96},{64,0},{96,32},{128,192},{160,224},{192,128},{224,1... | collective-permute-start | bytes 147464 | tf_op jit(solution)/shard_map/ppermute | solution.py:377
  151.6 5.7 %collective-permute-start.20 = (f32[96,128]{1,0:T(8,128)S(1)}, f32[96,128]{1,0:T(8,128)S(1)}, u32[]{:S(2)}, u32[]{:S(2)}) collective-permute-start(f32[96,128]{1,0:T(8,128)S(1)} %add_add_fusion), channel_id=1, source_target_pairs={{0,32},{32,0},{64,96},{96,64},{128,160},{160,128},{192,224},{224,1... | collective-permute-start | bytes 147464 | tf_op jit(solution)/shard_map/ppermute | solution.py:377
